TPU v7x, 32 devices: a whole 2x2x4 slice. The times are simulated.
32 devices in a mesh: leaf: 8 (over z, x), sub: 4 (over y, core).
Axes of the slice: x: 2, y: 2, z: 4, core: 2. Of those that a mesh axis runs over, the one named last changes fastest.
Arguments:
- points: bfloat16 [131072, 64], P(('leaf', 'sub')), may hold values from -6 to 6
- probes: bfloat16 [131072, 128], P(('leaf', 'sub')), may hold values from -6 to 6
- order: int32 [131072], P(('leaf', 'sub')), may hold values from 0 to 511, as said below
- near_lists: int32 [256, 12], P(('leaf', 'sub')), may hold values from 0 to 255, as said below
- near_counts: int32 [256], P(('leaf', 'sub')), may hold values from 1 to 12, as said below
- leaf_sets: int32 [256, 128], P(('leaf', 'sub')), may hold values from 0 to 511, as said below
- merge_sets: int32 [255, 128], replicated, may hold values from 0 to 255, as said below
Outputs:
- near_samples: float32 [131072, 128], P(('leaf', 'sub'))
- root_samples: float32 [16384], P(('leaf', 'sub'))
Inputs may be any that keep to these rules, and one draw needn't show every extreme that they name: `order`: the 512 entries of each leaf block are a permutation of 0 to 511. `near_lists`: for block g of shard i = g // 32: entry 0 is g; entries 1 to near_counts[g] - 1 are distinct blocks other than g within i * 32 - 8 to (i + 1) * 32 + 7; entries from near_counts[g] on equal g. `near_counts`: some block among the first sixteen of the aligned sixteens of blocks has 12 entries. `leaf_sets`: each row holds distinct values. `merge_sets`: each row holds distinct values; row m - 1 belongs to the node whose two children meet at block m.
All inputs are finite; a program needn't handle non-finite values.
Results may differ from a plain program's by a relative error of at most 0.0029.
Values may be sent and summed in bfloat16 or wider, within the bound.
No kernel may reach another device: no remote copies, remote signals or barrier semaphores. Data moves between devices by JAX's collectives and lax.ppermute only.
A program may use at most 128 MiB of HBM per device.

v0:
```python
import functools

import jax
import jax.numpy as jnp
from jax import lax
from jax.experimental import pallas as pl
from jax.experimental.pallas import tpu as pltpu
from jax.sharding import PartitionSpec as P

LANES = 128
PARTS = 3
VMEM_BYTES = 24 * 1024 * 1024
F32 = jnp.float32
BF16 = jnp.bfloat16


def dot(a, b):
    return jnp.dot(a, b, preferred_element_type=F32)


def dot_t(a, b):
    return lax.dot_general(a, b, (((0,), (0,)), ((), ())), preferred_element_type=F32)


def split(x):
    hi = x.astype(BF16)
    return hi, (x - hi.astype(F32)).astype(BF16)


def square_rows(pts):
    x = pts.astype(F32)
    total = jnp.sum(x * x, axis=0, keepdims=True)
    hi = total.astype(BF16).astype(F32)
    mid = (total - hi).astype(BF16).astype(F32)
    low = total - hi - mid
    row = lax.broadcasted_iota(jnp.int32, (16, pts.shape[1]), 0)
    ones = jnp.where(row < 2 * PARTS, 1.0, 0.0)
    return jnp.where(row == 0, hi, jnp.where(row == 1, mid, jnp.where(row == 2, low, ones))).astype(BF16)


def form_map(dim, size):
    k = lax.broadcasted_iota(jnp.int32, (size, size), 0)
    j = lax.broadcasted_iota(jnp.int32, (size, size), 1)
    r = jnp.where((k == j) & (j < dim), 2.0 / dim, 0.0)
    r = jnp.where((j >= dim) & (j < dim + PARTS) & (k == j + PARTS), -1.0 / dim, r)
    r = jnp.where((j >= dim + PARTS) & (j < dim + 2 * PARTS) & (k == j - PARTS), -1.0 / dim, r)
    return r.astype(BF16)


def onehot_in(row, size):
    index = lax.broadcasted_iota(jnp.int32, (size, row.shape[1]), 0)
    return jnp.where(index == row, 1.0, 0.0).astype(BF16)


def column_of(row):
    return jnp.broadcast_to(row.astype(F32), (LANES, row.shape[1])).T


def onehot_out(column, size):
    lane = lax.broadcasted_iota(jnp.int32, column.shape, 1).astype(F32)
    return jnp.concatenate(
        [jnp.where(column == lane + float(i), 1.0, 0.0) for i in range(0, size, LANES)], axis=1
    )


def mix3(m, s):
    m_hi, m_lo = split(m)
    s_hi, s_lo = split(s)
    return dot(m_hi, s_hi) + (dot(m_hi, s_lo) + dot(m_lo, s_hi))


def order_kernel(points_t, order, probes, pack, rows):
    dim = points_t.shape[0]
    many, leaf = rows.shape[:2]
    held = dim + 16
    to_rows = form_map(dim, LANES)
    for b in range(many):
        picks = onehot_in(order[b], leaf)
        tree_t = dot(points_t[:, b * leaf : (b + 1) * leaf], picks).astype(BF16)
        pack[b, :leaf, :] = probes[b * leaf : (b + 1) * leaf, :]
        form = jnp.concatenate([tree_t, square_rows(tree_t)], axis=0)
        for i in range(leaf // LANES):
            pack[b, leaf + i * held : leaf + (i + 1) * held, :] = form[:, i * LANES : (i + 1) * LANES]
        form = jnp.concatenate([form, jnp.zeros((LANES - held, leaf), BF16)], axis=0)
        rows[b] = dot_t(form, to_rows).astype(BF16)


def order_call(points_t, order, probes, blocks):
    dim, npts = points_t.shape
    leaf = npts // blocks
    packed = leaf + leaf // LANES * (dim + 16)
    many = 4 if blocks % 4 == 0 else 1
    return pl.pallas_call(
        order_kernel,
        grid=(blocks // many,),
        in_specs=[
            pl.BlockSpec((dim, many * leaf), lambda b: (0, b)),
            pl.BlockSpec((many, 1, leaf), lambda b: (b, 0, 0)),
            pl.BlockSpec((many * leaf, LANES), lambda b: (b, 0)),
        ],
        out_specs=[
            pl.BlockSpec((many, packed, LANES), lambda b: (b, 0, 0)),
            pl.BlockSpec((many, leaf, LANES), lambda b: (b, 0, 0)),
        ],
        out_shape=[
            jax.ShapeDtypeStruct((blocks, packed, LANES), BF16),
            jax.ShapeDtypeStruct((blocks, leaf, LANES), BF16),
        ],
        compiler_params=pltpu.CompilerParams(vmem_limit_bytes=VMEM_BYTES),
        cost_estimate=pl.CostEstimate(
            flops=blocks * 2 * leaf * leaf * dim, bytes_accessed=10 * npts * LANES, transcendentals=0
        ),
        name="tree_order",
    )(points_t, order, probes)


def form_of(pack_block, leaf, dim):
    held = dim + 16
    columns = [
        pack_block[leaf + i * held : leaf + (i + 1) * held, :] for i in range(leaf // LANES)
    ]
    form = jnp.concatenate(columns, axis=1)
    return jnp.concatenate([form, jnp.zeros((LANES - held, leaf), BF16)], axis=0)


def condense(form, a_rows, chosen):
    size = form.shape[1]
    picks_out = onehot_out(column_of(chosen), size)
    new_rows = dot(picks_out.astype(BF16), a_rows).astype(BF16)
    new_form = dot(form, onehot_in(chosen, size)).astype(BF16)
    weights = jnp.exp(dot(new_rows, form))
    mixing = picks_out + weights / jnp.sum(weights, axis=1, keepdims=True)
    return new_form, new_rows, mixing


def local_tree_kernel(pack, rows, leaf_sets, merge_sets, out, *, dim):
    blocks, leaf = rows.shape[:2]
    first_block = (lax.axis_index("leaf") * lax.axis_size("sub") + lax.axis_index("sub")) * blocks

    nodes = []
    for b in range(blocks):
        form = form_of(pack.at[b], leaf, dim)
        new_form, new_rows, mixing = condense(form, rows[b], leaf_sets[b : b + 1, :])
        m_hi, m_lo = split(mixing)
        probes = pack[b, :leaf, :]
        nodes.append((new_form, new_rows, dot(m_hi, probes) + dot(m_lo, probes)))
    span = 1
    while len(nodes) > 1:
        merged = []
        for k in range(len(nodes) // 2):
            left, right = nodes[2 * k], nodes[2 * k + 1]
            chosen = merge_sets[pl.ds(first_block + (2 * k + 1) * span - 1, 1), :]
            new_form, new_rows, mixing = condense(
                jnp.concatenate([left[0], right[0]], axis=1),
                jnp.concatenate([left[1], right[1]], axis=0),
                chosen,
            )
            samples = mix3(mixing, jnp.concatenate([left[2], right[2]], axis=0))
            merged.append((new_form, new_rows, samples))
        nodes = merged
        span *= 2
    held = dim + 16
    out[:held, :] = nodes[0][0][:held, :].astype(F32)
    out[held:, :] = nodes[0][2]


def local_tree_call(pack, rows, leaf_sets, merge_sets, dim):
    blocks, leaf = rows.shape[:2]
    skel = leaf_sets.shape[1]
    return pl.pallas_call(
        functools.partial(local_tree_kernel, dim=dim),
        out_shape=jax.ShapeDtypeStruct((dim + 16 + skel, LANES), F32),
        compiler_params=pltpu.CompilerParams(vmem_limit_bytes=VMEM_BYTES),
        cost_estimate=pl.CostEstimate(
            flops=blocks * 8 * skel * leaf * LANES,
            bytes_accessed=6 * blocks * leaf * LANES,
            transcendentals=blocks * skel * leaf,
        ),
        name="local_tree",
    )(pack, rows, leaf_sets, merge_sets)


def merge_kernel(group, merge_sets, out, *, dim, span, base, piece):
    held = dim + 16
    count, size = group.shape[:2]
    skel = size - held
    to_rows = form_map(dim, LANES)
    first = lax.axis_index(base) * count if base else 0
    forms = [group[i, :held, :].astype(BF16) for i in range(count)]
    samples = [group[i, held:, :] for i in range(count)]
    while len(forms) > 1:
        first = first // 2
        new_forms, new_samples = [], []
        for k in range(len(forms) // 2):
            chosen = merge_sets[pl.ds((2 * (first + k) + 1) * span - 1, 1), :]
            form = jnp.concatenate(forms[2 * k : 2 * k + 2], axis=1)
            form = jnp.concatenate([form, jnp.zeros((LANES - held, 2 * skel), BF16)], axis=0)
            new_form = dot(form, onehot_in(chosen, 2 * skel)).astype(BF16)
            new_rows = dot_t(new_form, to_rows).astype(BF16)
            weights = jnp.exp(dot(new_rows, form))
            picks = onehot_out(column_of(chosen), 2 * skel)
            mixing = picks + weights / jnp.sum(weights, axis=1, keepdims=True)
            new_forms.append(new_form[:held])
            new_samples.append(mix3(mixing, jnp.concatenate(samples[2 * k : 2 * k + 2], axis=0)))
        forms, samples = new_forms, new_samples
        span *= 2
    if piece is None:
        out[:held, :] = forms[0].astype(F32)
        out[held:, :] = samples[0]
    elif piece == 0:
        out[...] = samples[0]
    else:
        me = lax.axis_index("leaf") * lax.axis_size("sub") + lax.axis_index("sub")
        column = lax.broadcasted_iota(jnp.int32, (piece, skel), 1)
        row = lax.broadcasted_iota(jnp.int32, (piece, skel), 0) + me * piece
        take = jnp.where(column == row, 1.0, 0.0).astype(BF16)
        hi, lo = split(samples[0])
        low = (samples[0] - hi.astype(F32) - lo.astype(F32)).astype(BF16)
        out[...] = dot(take, hi) + dot(take, lo) + dot(take, low)


def merge_call(group, merge_sets, dim, span, base, piece=None):
    count, size = group.shape[:2]
    skel = size - dim - 16
    rows = size if piece is None else (piece or skel)
    return pl.pallas_call(
        functools.partial(merge_kernel, dim=dim, span=span, base=base, piece=piece),
        out_shape=jax.ShapeDtypeStruct((rows, LANES), F32),
        compiler_params=pltpu.CompilerParams(vmem_limit_bytes=20 * 1024 * 1024),
        cost_estimate=pl.CostEstimate(
            flops=count * 16 * LANES**3,
            bytes_accessed=4 * count * size * LANES,
            transcendentals=2 * count * LANES**2,
        ),
        name="tree_merge",
    )(group, merge_sets)


def near_kernel(*refs, slots, dim, has_acc, last):
    lists, counts, rows = refs[:3]
    refs = refs[3:]
    if has_acc:
        acc_in, refs = refs[0], refs[1:]
    buffers = []
    for _, which in slots:
        number = max(which) + 1
        buffers.append(refs[:number])
        refs = refs[number:]
    out, packs, pair_list, sems = refs
    blocks, leaf = rows.shape[:2]
    near = lists.shape[1]
    window = blocks * lax.axis_size("sub")
    start = lax.axis_index("leaf") * window - blocks
    sub = lax.axis_index("sub")

    def place(table):
        value = jnp.int32(table[0])
        for i in range(1, len(table)):
            value = jnp.where(sub == i, jnp.int32(table[i]), value)
        return value

    copies = []
    for slot, (bases, which) in enumerate(slots):
        target = packs.at[pl.ds(slot * blocks, blocks)]
        held = place(which)
        for number, buffer in enumerate(buffers[slot]):
            copy = pltpu.make_async_copy(buffer, target, sems.at[slot])
            if len(buffers[slot]) == 1:
                copy.start()
            else:
                pl.when(held == number)(copy.start)
        copies.append(copy)
    starts = [place(bases) for bases, _ in slots]

    if has_acc:
        acc_copy = pltpu.make_async_copy(acc_in, out, sems.at[len(slots)])
        acc_copy.start()
    else:
        out[...] = jnp.zeros(out.shape, F32)

    def list_block(g, found):
        used = counts[g]

        def list_slot(s, found):
            source = lists[g, s] - start
            local = jnp.int32(-1)
            for slot, first in enumerate(starts):
                inside = (source >= first) & (source < first + blocks)
                local = jnp.where(inside, source - first + slot * blocks, local)
            pair_list[found] = g * (len(slots) * blocks) + local
            return found + jnp.where((local >= 0) & (s < used), 1, 0)

        return lax.fori_loop(0, near, list_slot, found, unroll=True)

    pairs = lax.fori_loop(0, blocks, list_block, jnp.int32(0))

    for copy in copies:
        copy.wait()
    if has_acc:
        acc_copy.wait()

    half = leaf // 2

    def add_pair(i):
        code = pair_list[i]
        g = code // (len(slots) * blocks)
        local = code - g * (len(slots) * blocks)
        form = form_of(packs.at[local], leaf, dim)
        probes = packs[local, :leaf, :]
        sums = []
        for r in range(0, leaf, half):
            weights = jnp.exp(dot(rows[g, r : r + half, :], form)).astype(BF16)
            sums.append(dot(weights, probes))
        return g, sums

    def add_pairs(i, carry):
        found = [add_pair(2 * i), add_pair(2 * i + 1)]
        for g, sums in found:
            for j, value in enumerate(sums):
                out[g, j * half : (j + 1) * half, :] += value
        return carry

    lax.fori_loop(0, pairs // 2, add_pairs, 0)

    @pl.when(pairs % 2 == 1)
    def _():
        g, sums = add_pair(pairs - 1)
        for j, value in enumerate(sums):
            out[g, j * half : (j + 1) * half, :] += value

    if last:
        out[...] = out[...] * (leaf ** -0.5)


def near_call(lists, counts, rows, acc, sets, dim, last, name):
    blocks, leaf = rows.shape[:2]
    buffers = [b for _, _, bufs in sets for b in bufs]
    slots = tuple((bases, which) for bases, which, _ in sets)
    packed = buffers[0].shape[1]
    smem = pl.BlockSpec(memory_space=pltpu.SMEM)
    vmem = pl.BlockSpec(memory_space=pltpu.VMEM)
    args = [lists, counts, rows] + ([acc] if acc is not None else []) + buffers
    specs = [smem, smem, vmem]
    specs += [pl.BlockSpec(memory_space=pl.ANY)] * (len(buffers) + (acc is not None))
    total = len(slots) * blocks
    near = lists.shape[1]
    pairs = total * blocks // 8
    return pl.pallas_call(
        functools.partial(
            near_kernel, slots=slots, dim=dim, has_acc=acc is not None, last=last
        ),
        in_specs=specs,
        out_specs=vmem,
        out_shape=jax.ShapeDtypeStruct((blocks, leaf, LANES), F32),
        scratch_shapes=[
            pltpu.VMEM((total, packed, LANES), BF16),
            pltpu.SMEM((blocks * near + 8,), jnp.int32),
            pltpu.SemaphoreType.DMA((len(slots) + 1,)),
        ],
        compiler_params=pltpu.CompilerParams(vmem_limit_bytes=VMEM_BYTES),
        cost_estimate=pl.CostEstimate(
            flops=pairs * 2 * leaf * leaf * 256,
            bytes_accessed=total * packed * LANES * 2 + blocks * leaf * LANES * 8,
            transcendentals=pairs * leaf * leaf,
        ),
        name=name,
    )(*args)


def on_device(points, probes, order, near_lists, near_counts, leaf_sets, merge_sets):
    leaf_count = lax.axis_size("leaf")
    sub_count = lax.axis_size("sub")
    blocks, skel = leaf_sets.shape
    npts, dim = points.shape
    leaf = npts // blocks
    axes = ("leaf", "sub")

    def send(x, routes):
        pairs = []
        for place in range(leaf_count):
            for from_sub, step, to_sub in routes:
                if 0 <= place + step < leaf_count:
                    pairs.append((place * sub_count + from_sub, (place + step) * sub_count + to_sub))
        return lax.ppermute(x, axes, pairs)

    swap = [(0, 0, 1), (1, 0, 0), (2, 0, 3), (3, 0, 2)]
    pack, rows = order_call(points.T, order.reshape(blocks, 1, leaf), probes, blocks)
    outer_across = send(pack, [(3, 0, 1), (0, 0, 2)])
    outer_next = send(pack, [(3, 1, 3), (0, -1, 0)])
    beside = send(pack, swap)

    node = local_tree_call(pack, rows, leaf_sets, merge_sets, dim)

    beside, node = lax.optimization_barrier((beside, node))
    group = lax.all_gather(node, "sub", axis=0)

    b = blocks
    own_base, beside_base = (b, 2 * b, 3 * b, 4 * b), (2 * b, b, 4 * b, 3 * b)
    early_base, early_beside_base = (5 * b, 4 * b, b, 0), (4 * b, 5 * b, 0, b)
    late_base, late_beside_base = (3 * b, 0, 5 * b, 2 * b), (0, 3 * b, 2 * b, 5 * b)
    single = (0, 0, 0, 0)
    acc = near_call(
        near_lists, near_counts, rows, None,
        [(own_base, single, [pack]), (beside_base, single, [beside])],
        dim, False, "near_first",
    )

    inner_pack, outer_across, outer_next, acc = lax.optimization_barrier(
        (pack, outer_across, outer_next, acc)
    )
    inner_across = send(inner_pack, [(2, 0, 0), (1, 0, 3)])
    forwarded = send(outer_across, [(1, 1, 1), (2, -1, 2)])
    place = lax.axis_index("sub")
    at_edge = (place == 0) | (place == sub_count - 1)
    early = jnp.where(at_edge, outer_next, outer_across)
    early_beside = send(early, swap)

    group, early = lax.optimization_barrier((group, early))
    node = merge_call(group, merge_sets, dim, blocks, "leaf")
    early_beside, node = lax.optimization_barrier((early_beside, node))
    group = lax.all_gather(node, "leaf", axis=0)
    acc = near_call(
        near_lists, near_counts, rows, acc,
        [(early_base, single, [early]), (early_beside_base, single, [early_beside])],
        dim, False, "near_second",
    )

    inner_across, forwarded, acc = lax.optimization_barrier((inner_across, forwarded, acc))
    late = jnp.where(at_edge, inner_across, forwarded)
    late_beside = send(late, swap)
    group, late = lax.optimization_barrier((group, late))
    piece = skel // (leaf_count * sub_count)
    node = merge_call(group, merge_sets, dim, blocks * sub_count, None, piece)
    if piece:
        root = node.reshape(-1)
    else:
        size = skel * LANES // (leaf_count * sub_count)
        rank = lax.axis_index("leaf") * sub_count + place
        root = lax.dynamic_slice_in_dim(node.reshape(-1), rank * size, size, 0)
    near = near_call(
        near_lists, near_counts, rows, acc,
        [(late_base, single, [late]), (late_beside_base, single, [late_beside])],
        dim, True, "near_last",
    )
    return near.reshape(npts, LANES), root


def solution(mesh):
    in_specs = (
        P(("leaf", "sub"), None),
        P(("leaf", "sub"), None),
        P(("leaf", "sub")),
        P(("leaf", "sub"), None),
        P(("leaf", "sub")),
        P(("leaf", "sub"), None),
        P(),
    )
    out_specs = (P(("leaf", "sub"), None), P(("leaf", "sub")))
    return jax.shard_map(
        on_device, mesh=mesh, in_specs=in_specs, out_specs=out_specs, check_vma=False
    )
```

profile of v0, /device:TPU:4, one launch (start us, length us, event | category | flops | bytes accessed | tf_op | source)
XLA Modules:
  0.0 127.6 jit_solution(6818143436684572507)
XLA Ops:
  0.6 1.2 copy-done
  1.9 1.0 copy-done.1
  2.9 0.7 copy-done.4
  3.6 2.6 %tree_order.1 = (bf16[8,832,128]{2,1,0:T(8,128)(2,1)S(1)}, bf16[8,512,128]{2,1,0:T(8,128)(2,1)S(1)}) custom-call(bf16[64,4096]{1,0:T(8,128)(2,1)S(1)} %bitcast.8, s32[8,1,512]{2,1,0:T(1,128)S(1)} %bitcast.9, bf16[4096,128]{1,0:T(8,128)(2,1)S(1)} %copy-done), custom_call_target="tpu_custom_call" | custom-call | flops 268435456 | bytes 5242880 | tf_op jit(solution)/shard_map/tree_order/pallas_call | solution.py:93
  6.3 0.0 copy-start.5
  6.3 0.1 collective-permute-start.2
  6.4 1.9 %collective-permute-start.1 = (bf16[8,832,128]{2,1,0:T(8,128)(2,1)S(1)}, bf16[8,832,128]{2,1,0:T(8,128)(2,1)}, u32[]{:S(2)}, u32[]{:S(2)}) collective-permute-start(bf16[8,832,128]{2,1,0:T(8,128)(2,1)S(1)} %get-tuple-element.22.pack.refs_3_), channel_id=1, source_target_pairs={{3,7},{7,11},{4,0},{11,15},{8,4},{15,19},{12,8},{19,23},{16,12},{2... | collective-permute-start | bytes 5111816 | tf_op jit(solution)/shard_map/ppermute | solution.py:384
  8.2 1.3 %collective-permute-start = (bf16[8,832,128]{2,1,0:T(8,128)(2,1)S(1)}, bf16[8,832,128]{2,1,0:T(8,128)(2,1)}, u32[]{:S(2)}, u32[]{:S(2)}) collective-permute-start(bf16[8,832,128]{2,1,0:T(8,128)(2,1)S(1)} %get-tuple-element.22.pack.refs_3_), channel_id=1, source_target_pairs={{3,1},{0,2},{7,5},{4,6},{11,9},{8,10},{15,13},{12,14},{19,17},{16,... | collective-permute-start | bytes 5111816 | tf_op jit(solution)/shard_map/ppermute | solution.py:384
  9.5 0.9 copy-done.2
  10.4 0.7 copy-done.6
  11.1 6.5 %local_tree.1 = f32[208,128]{1,0:T(8,128)S(1)} custom-call(bf16[8,832,128]{2,1,0:T(8,128)(2,1)S(1)} %get-tuple-element.22.pack.refs_3_, bf16[8,512,128]{2,1,0:T(8,128)(2,1)S(1)} %get-tuple-element.19.rows.refs_2_, s32[8,128]{1,0:T(8,128)S(1)} %copy-done.6, s32[255,128]{1,0:T(8,128)S(1)} %copy-done.2), custom_call_target="tpu_custom_call" | custom-call | flops 536870912 | bytes 3145728 | tf_op jit(solution)/shard_map/local_tree/pallas_call | solution.py:170
  17.7 15.6 %near_first.1.refs_3_ = f32[8,512,128]{2,1,0:T(8,128)S(1)} custom-call(s32[8,12]{1,0:T(8,128)S(1)} %copy-done.5, s32[8]{0:T(128)S(1)} %copy-done.7, bf16[8,512,128]{2,1,0:T(8,128)(2,1)S(1)} %get-tuple-element.19.rows.refs_2_, bf16[8,832,128]{2,1,0:T(8,128)(2,1)S(1)} %get-tuple-element.22.pack.refs_3_, bf16[8,832,128]{2,1,0:T(8,128)(2,1)} %collective-permute-done.2.refs_4_), custom_call_target="tpu_custom_call" | custom-call | flops 2147483648 | bytes 7602176 | tf_op jit(solution)/shard_map/near_first/pallas_call | solution.py:348
  33.3 1.7 %broadcast_select_fusion.1.refs_4_ = bf16[8,832,128]{2,1,0:T(8,128)(2,1)S(1)} fusion(bf16[8,832,128]{2,1,0:T(8,128)(2,1)} %collective-permute-done.1, bf16[8,832,128]{2,1,0:T(8,128)(2,1)} %collective-permute-done, pred[]{:T(512)S(6)} %or.3), kind=kLoop, calls=%fused_computation.1 | loop fusion | flops 851968 | bytes 5111809 | tf_op jit(solution)/shard_map/jit(_where)/select_n | solution.py:415
  35.0 1.1 collective-permute-start.5
  36.1 2.8 %collective-permute-start.3 = (bf16[8,832,128]{2,1,0:T(8,128)(2,1)S(1)}, bf16[8,832,128]{2,1,0:T(8,128)(2,1)S(1)}, u32[]{:S(2)}, u32[]{:S(2)}) collective-permute-start(bf16[8,832,128]{2,1,0:T(8,128)(2,1)S(1)} %get-tuple-element.22.pack.refs_3_), channel_id=1, source_target_pairs={{2,0},{1,3},{6,4},{5,7},{10,8},{9,11},{14,12},{13,15},{18,16},{17,... | collective-permute-start | bytes 5111816 | tf_op jit(solution)/shard_map/ppermute | solution.py:384
  38.9 1.3 %collective-permute-start.4 = (bf16[8,832,128]{2,1,0:T(8,128)(2,1)}, bf16[8,832,128]{2,1,0:T(8,128)(2,1)S(1)}, u32[]{:S(2)}, u32[]{:S(2)}) collective-permute-start(bf16[8,832,128]{2,1,0:T(8,128)(2,1)} %collective-permute-done), channel_id=1, source_target_pairs={{1,5},{5,9},{6,2},{9,13},{10,6},{13,17},{14,10},{17,21},{18,14},{2... | collective-permute-start | bytes 5111816 | tf_op jit(solution)/shard_map/ppermute | solution.py:384
  40.2 21.8 %all-gather = f32[832,128]{1,0:T(8,128)S(1)} all-gather(f32[208,128]{1,0:T(8,128)S(1)} %local_tree.1), channel_id=2, replica_groups=mesh['leaf'=8,'sub'=4] {'sub'}, dimensions={0}, use_global_device_ids=true | all-gather | bytes 532480 | tf_op jit(solution)/shard_map/all_gather | solution.py:395
  62.0 2.0 %tree_merge.2 = f32[208,128]{1,0:T(8,128)S(1)} custom-call(f32[4,208,128]{2,1,0:T(8,128)S(1)} %bitcast.6, s32[255,128]{1,0:T(8,128)S(1)} %copy-done.3), custom_call_target="tpu_custom_call" | custom-call | flops 134217728 | bytes 425984 | tf_op jit(solution)/shard_map/tree_merge/pallas_call | solution.py:226
  64.0 5.0 %near_second.1.refs_3_ = f32[8,512,128]{2,1,0:T(8,128)S(1)} custom-call(s32[8,12]{1,0:T(8,128)S(1)} %copy-done.5, s32[8]{0:T(128)S(1)} %copy-done.7, bf16[8,512,128]{2,1,0:T(8,128)(2,1)S(1)} %get-tuple-element.19.rows.refs_2_, f32[8,512,128]{2,1,0:T(8,128)S(1)} %near_first.1.refs_3_, bf16[8,832,128]{2,1,0:T(8,128)(2,1)S(1)} %broadcast_select_fusion.1.refs_4_, ...), custom_call_target="tpu_custom_call" | custom-call | flops 2147483648 | bytes 7602176 | tf_op jit(solution)/shard_map/near_second/pallas_call | solution.py:348
  69.0 0.2 broadcast_select_fusion.refs_4_
  69.2 0.1 collective-permute-start.6
  69.3 39.7 %all-gather.1 = f32[1664,128]{1,0:T(8,128)S(1)} all-gather(f32[208,128]{1,0:T(8,128)S(1)} %tree_merge.2), channel_id=3, replica_groups=mesh['leaf'=8,'sub'=4] {'leaf'}, dimensions={0}, use_global_device_ids=true | all-gather | bytes 958464 | tf_op jit(solution)/shard_map/all_gather | solution.py:421
  109.1 5.1 %tree_merge.3 = f32[4,128]{1,0:T(4,128)} custom-call(f32[8,208,128]{2,1,0:T(8,128)S(1)} %bitcast.7, s32[255,128]{1,0:T(8,128)S(1)} %copy-done.3), custom_call_target="tpu_custom_call" | custom-call | flops 268435456 | bytes 851968 | tf_op jit(solution)/shard_map/tree_merge/pallas_call | solution.py:226
  114.2 13.2 %near_last.1 = f32[8,512,128]{2,1,0:T(8,128)} custom-call(s32[8,12]{1,0:T(8,128)S(1)} %copy-done.5, s32[8]{0:T(128)S(1)} %copy-done.7, bf16[8,512,128]{2,1,0:T(8,128)(2,1)S(1)} %get-tuple-element.19.rows.refs_2_, f32[8,512,128]{2,1,0:T(8,128)S(1)} %near_second.1.refs_3_, bf16[8,832,128]{2,1,0:T(8,128)(2,1)S(1)} %broadcast_select_fusion.refs_4_, ...), custom_call_target="tpu_custom_call" | custom-call | flops 2147483648 | bytes 7602176 | tf_op jit(solution)/shard_map/near_last/pallas_call | solution.py:348
  (17 shorter events, 0.0 us)
Async XLA Ops:
  0.6 1.2 copy-start
  1.9 1.0 copy-start.1
  2.9 0.7 copy-start.4
  6.3 11.4 %copy-start.5 = (s32[8,12]{1,0:T(8,128)S(1)}, s32[8,12]{1,0:T(8,128)}, u32[]{:S(2)}) copy-start(s32[8,12]{1,0:T(8,128)} %refs_0_.5) | copy-start | bytes 1156
  6.3 11.4 %copy-start.7 = (s32[8]{0:T(128)S(1)}, s32[8]{0:T(128)}, u32[]{:S(2)}) copy-start(s32[8]{0:T(128)} %refs_1_.5) | copy-start | bytes 100
  6.3 11.3 %collective-permute-start.2 = (bf16[8,832,128]{2,1,0:T(8,128)(2,1)S(1)}, bf16[8,832,128]{2,1,0:T(8,128)(2,1)}, u32[]{:S(2)}, u32[]{:S(2)}) collective-permute-start(bf16[8,832,128]{2,1,0:T(8,128)(2,1)S(1)} %get-tuple-element.22.pack.refs_3_), channel_id=1, source_target_pairs={{0,1},{1,0},{2,3},{3,2},{4,5},{5,4},{6,7},{7,6},{8,9},{9,8},{10,11... | collective-permute-start | bytes 5111816 | tf_op jit(solution)/shard_map/ppermute | solution.py:384
  6.4 26.9 %collective-permute-start.1 = (bf16[8,832,128]{2,1,0:T(8,128)(2,1)S(1)}, bf16[8,832,128]{2,1,0:T(8,128)(2,1)}, u32[]{:S(2)}, u32[]{:S(2)}) collective-permute-start(bf16[8,832,128]{2,1,0:T(8,128)(2,1)S(1)} %get-tuple-element.22.pack.refs_3_), channel_id=1, source_target_pairs={{3,7},{7,11},{4,0},{11,15},{8,4},{15,19},{12,8},{19,23},{16,12},{2... | collective-permute-start | bytes 5111816 | tf_op jit(solution)/shard_map/ppermute | solution.py:384
  8.2 25.1 %collective-permute-start = (bf16[8,832,128]{2,1,0:T(8,128)(2,1)S(1)}, bf16[8,832,128]{2,1,0:T(8,128)(2,1)}, u32[]{:S(2)}, u32[]{:S(2)}) collective-permute-start(bf16[8,832,128]{2,1,0:T(8,128)(2,1)S(1)} %get-tuple-element.22.pack.refs_3_), channel_id=1, source_target_pairs={{3,1},{0,2},{7,5},{4,6},{11,9},{8,10},{15,13},{12,14},{19,17},{16,... | collective-permute-start | bytes 5111816 | tf_op jit(solution)/shard_map/ppermute | solution.py:384
  9.5 0.9 copy-start.2
  10.4 0.7 copy-start.6
  33.3 28.7 %copy-start.3 = (s32[255,128]{1,0:T(8,128)S(1)}, s32[255,128]{1,0:T(8,128)}, u32[]{:S(2)}) copy-start(s32[255,128]{1,0:T(8,128)} %merge_sets.5) | copy-start | bytes 391684
  35.0 29.0 %collective-permute-start.5 = (bf16[8,832,128]{2,1,0:T(8,128)(2,1)S(1)}, bf16[8,832,128]{2,1,0:T(8,128)(2,1)S(1)}, u32[]{:S(2)}, u32[]{:S(2)}) collective-permute-start(bf16[8,832,128]{2,1,0:T(8,128)(2,1)S(1)} %broadcast_select_fusion.1.refs_4_), channel_id=1, source_target_pairs={{0,1},{1,0},{2,3},{3,2},{4,5},{5,4},{6,7},{7,6},{8,9},{9,8},{10,11... | collective-permute-start | bytes 5111816 | tf_op jit(solution)/shard_map/ppermute | solution.py:384
  36.1 32.9 %collective-permute-start.3 = (bf16[8,832,128]{2,1,0:T(8,128)(2,1)S(1)}, bf16[8,832,128]{2,1,0:T(8,128)(2,1)S(1)}, u32[]{:S(2)}, u32[]{:S(2)}) collective-permute-start(bf16[8,832,128]{2,1,0:T(8,128)(2,1)S(1)} %get-tuple-element.22.pack.refs_3_), channel_id=1, source_target_pairs={{2,0},{1,3},{6,4},{5,7},{10,8},{9,11},{14,12},{13,15},{18,16},{17,... | collective-permute-start | bytes 5111816 | tf_op jit(solution)/shard_map/ppermute | solution.py:384
  38.9 30.1 %collective-permute-start.4 = (bf16[8,832,128]{2,1,0:T(8,128)(2,1)}, bf16[8,832,128]{2,1,0:T(8,128)(2,1)S(1)}, u32[]{:S(2)}, u32[]{:S(2)}) collective-permute-start(bf16[8,832,128]{2,1,0:T(8,128)(2,1)} %collective-permute-done), channel_id=1, source_target_pairs={{1,5},{5,9},{6,2},{9,13},{10,6},{13,17},{14,10},{17,21},{18,14},{2... | collective-permute-start | bytes 5111816 | tf_op jit(solution)/shard_map/ppermute | solution.py:384
  69.2 45.0 %collective-permute-start.6 = (bf16[8,832,128]{2,1,0:T(8,128)(2,1)S(1)}, bf16[8,832,128]{2,1,0:T(8,128)(2,1)S(1)}, u32[]{:S(2)}, u32[]{:S(2)}) collective-permute-start(bf16[8,832,128]{2,1,0:T(8,128)(2,1)S(1)} %broadcast_select_fusion.refs_4_), channel_id=1, source_target_pairs={{0,1},{1,0},{2,3},{3,2},{4,5},{5,4},{6,7},{7,6},{8,9},{9,8},{10,11... | collective-permute-start | bytes 5111816 | tf_op jit(solution)/shard_map/ppermute | solution.py:384
where the time goes:
time: 127 us; the launch traced here: 128 us
  blocking collectives  61.5 us (48%)
  Pallas kernels  50.1 us (39%)
  starting transfers between devices  8.45 us (7%)
  local copies, waits for them, and re-layouts  4.58 us (4%)
  other arithmetic  1.86 us (1%)
    all_gather x1, blocking collectives, on_device(): group = lax.all_gather(node, 'leaf', axis=0)  39.7 us
    pallas_call x3, Pallas kernels, near_call(): pl.pallas_call(functools.partial(near_kernel, slots=slots, dim=dim, has_a...  33.9 us
    all_gather x1, blocking collectives, on_device(): group = lax.all_gather(node, 'sub', axis=0)  21.8 us
    ppermute x7, starting transfers between devices, send(): return lax.ppermute(x, axes, pairs)  8.45 us
    pallas_call x2, Pallas kernels, merge_call(): pl.pallas_call(functools.partial(merge_kernel, dim=dim, span=span, base=b...  7.12 us
    pallas_call x1, Pallas kernels, local_tree_call(): pl.pallas_call(functools.partial(local_tree_kernel, dim=dim), out_shape=j...  6.5 us
    unnamed x16, local copies, waits for them, and re-layouts  4.58 us
    pallas_call x1, Pallas kernels, order_call(): pl.pallas_call(order_kernel, grid=(blocks // many,), in_specs=[pl.BlockSp...  2.65 us
  transfers between devices with their start and end apart: 7, of which 0 were waited for; matrix products, arithmetic and copies ran while one was open for 0% of the time, Pallas kernels for 27%

commit v1 on v0

--- a/solution.py
+++ b/solution.py
@@ -69,42 +69,55 @@
     return dot(m_hi, s_hi) + (dot(m_hi, s_lo) + dot(m_lo, s_hi))
 
 
-def order_kernel(points_t, order, probes, pack, rows):
+def order_kernel(points_t, order, probes, pack, rows, points_in, order_in, sems):
     dim = points_t.shape[0]
     many, leaf = rows.shape[:2]
     held = dim + 16
+    order_copy = pltpu.make_async_copy(order, order_in, sems.at[0])
+    order_copy.start()
+    point_copies, probe_copies = [], []
+    for b in range(many):
+        span = pl.ds(b * leaf, leaf)
+        copy = pltpu.make_async_copy(points_t.at[:, span], points_in.at[b], sems.at[1 + b])
+        copy.start()
+        point_copies.append(copy)
+    for b in range(many):
+        span = pl.ds(b * leaf, leaf)
+        copy = pltpu.make_async_copy(
+            probes.at[span], pack.at[b, pl.ds(0, leaf)], sems.at[1 + many + b]
+        )
+        copy.start()
+        probe_copies.append(copy)
     to_rows = form_map(dim, LANES)
+    order_copy.wait()
     for b in range(many):
-        picks = onehot_in(order[b], leaf)
-        tree_t = dot(points_t[:, b * leaf : (b + 1) * leaf], picks).astype(BF16)
-        pack[b, :leaf, :] = probes[b * leaf : (b + 1) * leaf, :]
+        picks = onehot_in(order_in[b], leaf)
+        point_copies[b].wait()
+        tree_t = dot(points_in[b], picks).astype(BF16)
         form = jnp.concatenate([tree_t, square_rows(tree_t)], axis=0)
         for i in range(leaf // LANES):
             pack[b, leaf + i * held : leaf + (i + 1) * held, :] = form[:, i * LANES : (i + 1) * LANES]
         form = jnp.concatenate([form, jnp.zeros((LANES - held, leaf), BF16)], axis=0)
         rows[b] = dot_t(form, to_rows).astype(BF16)
+    for copy in probe_copies:
+        copy.wait()
 
 
 def order_call(points_t, order, probes, blocks):
     dim, npts = points_t.shape
     leaf = npts // blocks
     packed = leaf + leaf // LANES * (dim + 16)
-    many = 4 if blocks % 4 == 0 else 1
     return pl.pallas_call(
         order_kernel,
-        grid=(blocks // many,),
-        in_specs=[
-            pl.BlockSpec((dim, many * leaf), lambda b: (0, b)),
-            pl.BlockSpec((many, 1, leaf), lambda b: (b, 0, 0)),
-            pl.BlockSpec((many * leaf, LANES), lambda b: (b, 0)),
-        ],
-        out_specs=[
-            pl.BlockSpec((many, packed, LANES), lambda b: (b, 0, 0)),
-            pl.BlockSpec((many, leaf, LANES), lambda b: (b, 0, 0)),
-        ],
+        in_specs=[pl.BlockSpec(memory_space=pltpu.HBM)] * 3,
         out_shape=[
             jax.ShapeDtypeStruct((blocks, packed, LANES), BF16),
             jax.ShapeDtypeStruct((blocks, leaf, LANES), BF16),
+        ],
+        scratch_shapes=[
+            pltpu.VMEM((blocks, dim, leaf), BF16),
+            pltpu.VMEM((blocks, 1, leaf), jnp.int32),
+            pltpu.SemaphoreType.DMA((1 + 2 * blocks,)),
         ],
         compiler_params=pltpu.CompilerParams(vmem_limit_bytes=VMEM_BYTES),
         cost_estimate=pl.CostEstimate(
@@ -133,8 +146,13 @@
     return new_form, new_rows, mixing
 
 
-def local_tree_kernel(pack, rows, leaf_sets, merge_sets, out, *, dim):
+def local_tree_kernel(pack, rows, leaf_sets_in, merge_sets_in, out, leaf_sets, merge_sets, sems, *, dim):
     blocks, leaf = rows.shape[:2]
+    leaf_copy = pltpu.make_async_copy(leaf_sets_in, leaf_sets, sems.at[0])
+    merge_copy = pltpu.make_async_copy(merge_sets_in, merge_sets, sems.at[1])
+    leaf_copy.start()
+    merge_copy.start()
+    leaf_copy.wait()
     first_block = (lax.axis_index("leaf") * lax.axis_size("sub") + lax.axis_index("sub")) * blocks
 
     nodes = []
@@ -145,6 +163,7 @@
         probes = pack[b, :leaf, :]
         nodes.append((new_form, new_rows, dot(m_hi, probes) + dot(m_lo, probes)))
     span = 1
+    merge_copy.wait()
     while len(nodes) > 1:
         merged = []
         for k in range(len(nodes) // 2):
@@ -169,7 +188,14 @@
     skel = leaf_sets.shape[1]
     return pl.pallas_call(
         functools.partial(local_tree_kernel, dim=dim),
+        in_specs=[pl.BlockSpec(memory_space=pltpu.VMEM)] * 2
+        + [pl.BlockSpec(memory_space=pltpu.HBM)] * 2,
         out_shape=jax.ShapeDtypeStruct((dim + 16 + skel, LANES), F32),
+        scratch_shapes=[
+            pltpu.VMEM(leaf_sets.shape, jnp.int32),
+            pltpu.VMEM(merge_sets.shape, jnp.int32),
+            pltpu.SemaphoreType.DMA((2,)),
+        ],
         compiler_params=pltpu.CompilerParams(vmem_limit_bytes=VMEM_BYTES),
         cost_estimate=pl.CostEstimate(
             flops=blocks * 8 * skel * leaf * LANES,
@@ -180,14 +206,25 @@
     )(pack, rows, leaf_sets, merge_sets)
 
 
-def merge_kernel(group, merge_sets, out, *, dim, span, base, piece):
+def merge_kernel(*refs, dim, blocks, shift, piece):
+    merge_sets_in, out, group, merge_sets, sem = refs[-5:]
+    parts = refs[:-5]
+    count, size = group.shape[:2]
+    copy = pltpu.make_async_copy(merge_sets_in, merge_sets, sem)
+    copy.start()
     held = dim + 16
-    count, size = group.shape[:2]
     skel = size - held
+    rank = lax.axis_index("leaf") * lax.axis_size("sub") + lax.axis_index("sub")
+    unit = lax.shift_right_logical(rank, shift)
+    place = unit & (count - 1)
+    first = unit - place
+    span = blocks << shift
+    for d, part in enumerate(parts):
+        group[place ^ d] = part[...]
     to_rows = form_map(dim, LANES)
-    first = lax.axis_index(base) * count if base else 0
     forms = [group[i, :held, :].astype(BF16) for i in range(count)]
     samples = [group[i, held:, :] for i in range(count)]
+    copy.wait()
     while len(forms) > 1:
         first = first // 2
         new_forms, new_samples = [], []
@@ -210,30 +247,37 @@
     elif piece == 0:
         out[...] = samples[0]
     else:
-        me = lax.axis_index("leaf") * lax.axis_size("sub") + lax.axis_index("sub")
         column = lax.broadcasted_iota(jnp.int32, (piece, skel), 1)
-        row = lax.broadcasted_iota(jnp.int32, (piece, skel), 0) + me * piece
+        row = lax.broadcasted_iota(jnp.int32, (piece, skel), 0) + rank * piece
         take = jnp.where(column == row, 1.0, 0.0).astype(BF16)
         hi, lo = split(samples[0])
         low = (samples[0] - hi.astype(F32) - lo.astype(F32)).astype(BF16)
         out[...] = dot(take, hi) + dot(take, lo) + dot(take, low)
 
 
-def merge_call(group, merge_sets, dim, span, base, piece=None):
-    count, size = group.shape[:2]
+def merge_call(parts, merge_sets, dim, blocks, shift, piece=None):
+    count = len(parts)
+    size = parts[0].shape[0]
     skel = size - dim - 16
     rows = size if piece is None else (piece or skel)
     return pl.pallas_call(
-        functools.partial(merge_kernel, dim=dim, span=span, base=base, piece=piece),
+        functools.partial(merge_kernel, dim=dim, blocks=blocks, shift=shift, piece=piece),
+        in_specs=[pl.BlockSpec(memory_space=pltpu.VMEM)] * count
+        + [pl.BlockSpec(memory_space=pltpu.HBM)],
         out_shape=jax.ShapeDtypeStruct((rows, LANES), F32),
-        compiler_params=pltpu.CompilerParams(vmem_limit_bytes=20 * 1024 * 1024),
+        scratch_shapes=[
+            pltpu.VMEM((count, size, LANES), F32),
+            pltpu.VMEM(merge_sets.shape, jnp.int32),
+            pltpu.SemaphoreType.DMA(()),
+        ],
+        compiler_params=pltpu.CompilerParams(vmem_limit_bytes=16 * 1024 * 1024),
         cost_estimate=pl.CostEstimate(
             flops=count * 16 * LANES**3,
             bytes_accessed=4 * count * size * LANES,
             transcendentals=2 * count * LANES**2,
         ),
         name="tree_merge",
-    )(group, merge_sets)
+    )(*parts, merge_sets)
 
 
 def near_kernel(*refs, slots, dim, has_acc, last):
@@ -307,26 +351,25 @@
         local = code - g * (len(slots) * blocks)
         form = form_of(packs.at[local], leaf, dim)
         probes = packs[local, :leaf, :]
-        sums = []
-        for r in range(0, leaf, half):
-            weights = jnp.exp(dot(rows[g, r : r + half, :], form)).astype(BF16)
-            sums.append(dot(weights, probes))
-        return g, sums
+        total = None
+        for c in range(0, leaf, half):
+            weights = jnp.exp(dot(rows[g], form[:, c : c + half])).astype(BF16)
+            term = dot(weights, probes[c : c + half])
+            total = term if total is None else total + term
+        return g, total
 
     def add_pairs(i, carry):
         found = [add_pair(2 * i), add_pair(2 * i + 1)]
-        for g, sums in found:
-            for j, value in enumerate(sums):
-                out[g, j * half : (j + 1) * half, :] += value
+        for g, total in found:
+            out[g] += total
         return carry
 
     lax.fori_loop(0, pairs // 2, add_pairs, 0)
 
     @pl.when(pairs % 2 == 1)
     def _():
-        g, sums = add_pair(pairs - 1)
-        for j, value in enumerate(sums):
-            out[g, j * half : (j + 1) * half, :] += value
+        g, total = add_pair(pairs - 1)
+        out[g] += total
 
     if last:
         out[...] = out[...] * (leaf ** -0.5)
@@ -391,57 +434,77 @@
 
     node = local_tree_call(pack, rows, leaf_sets, merge_sets, dim)
 
-    beside, node = lax.optimization_barrier((beside, node))
-    group = lax.all_gather(node, "sub", axis=0)
+    count = leaf_count * sub_count
+    bits = count.bit_length() - 1
+    sub_bits = sub_count.bit_length() - 1
+
+    def exchange(x, shift, stage_bits):
+        parts = [x]
+        for d in range(1, 1 << stage_bits):
+            parts.append(lax.ppermute(x, axes, [(i, i ^ (d << shift)) for i in range(count)]))
+        return parts
 
     b = blocks
     own_base, beside_base = (b, 2 * b, 3 * b, 4 * b), (2 * b, b, 4 * b, 3 * b)
     early_base, early_beside_base = (5 * b, 4 * b, b, 0), (4 * b, 5 * b, 0, b)
     late_base, late_beside_base = (3 * b, 0, 5 * b, 2 * b), (0, 3 * b, 2 * b, 5 * b)
-    single = (0, 0, 0, 0)
+    single, edge_first, edge_second = (0, 0, 0, 0), (0, 1, 1, 0), (1, 0, 0, 1)
+    from_edge, from_inner = [(0, 0, 1), (3, 0, 2)], [(1, 0, 0), (2, 0, 3)]
+
+    def tie(*values):
+        return lax.optimization_barrier(values)
+
+    beside, node = tie(beside, node)
+    parts = exchange(node, 0, sub_bits)
     acc = near_call(
         near_lists, near_counts, rows, None,
         [(own_base, single, [pack]), (beside_base, single, [beside])],
         dim, False, "near_first",
     )
 
-    inner_pack, outer_across, outer_next, acc = lax.optimization_barrier(
-        (pack, outer_across, outer_next, acc)
-    )
+    *parts, acc = tie(*parts, acc)
+    node = merge_call(parts, merge_sets, dim, blocks, 0)
+    inner_pack, outer_across, outer_next, node = tie(pack, outer_across, outer_next, node)
+    shift, stage_bits = sub_bits, min(2, bits - sub_bits)
+    parts = exchange(node, shift, stage_bits)
     inner_across = send(inner_pack, [(2, 0, 0), (1, 0, 3)])
     forwarded = send(outer_across, [(1, 1, 1), (2, -1, 2)])
-    place = lax.axis_index("sub")
-    at_edge = (place == 0) | (place == sub_count - 1)
-    early = jnp.where(at_edge, outer_next, outer_across)
-    early_beside = send(early, swap)
-
-    group, early = lax.optimization_barrier((group, early))
-    node = merge_call(group, merge_sets, dim, blocks, "leaf")
-    early_beside, node = lax.optimization_barrier((early_beside, node))
-    group = lax.all_gather(node, "leaf", axis=0)
+    next_beside = send(outer_next, from_edge)
+    across_beside = send(outer_across, from_inner)
     acc = near_call(
         near_lists, near_counts, rows, acc,
-        [(early_base, single, [early]), (early_beside_base, single, [early_beside])],
+        [
+            (early_base, edge_first, [outer_next, outer_across]),
+            (early_beside_base, edge_second, [next_beside, across_beside]),
+        ],
         dim, False, "near_second",
     )
 
-    inner_across, forwarded, acc = lax.optimization_barrier((inner_across, forwarded, acc))
-    late = jnp.where(at_edge, inner_across, forwarded)
-    late_beside = send(late, swap)
-    group, late = lax.optimization_barrier((group, late))
-    piece = skel // (leaf_count * sub_count)
-    node = merge_call(group, merge_sets, dim, blocks * sub_count, None, piece)
+    *parts, inner_across, forwarded, acc = tie(*parts, inner_across, forwarded, acc)
+    inner_beside = send(inner_across, from_edge)
+    forwarded_beside = send(forwarded, from_inner)
+    node = merge_call(parts, merge_sets, dim, blocks, shift)
+    shift += stage_bits
+    inner_beside, forwarded_beside, node = tie(inner_beside, forwarded_beside, node)
+    parts = exchange(node, shift, bits - shift)
+    near = near_call(
+        near_lists, near_counts, rows, acc,
+        [
+            (late_base, edge_first, [inner_across, forwarded]),
+            (late_beside_base, edge_second, [inner_beside, forwarded_beside]),
+        ],
+        dim, True, "near_last",
+    )
+
+    *parts, near = tie(*parts, near)
+    piece = skel // count
+    node = merge_call(parts, merge_sets, dim, blocks, shift, piece)
     if piece:
         root = node.reshape(-1)
     else:
-        size = skel * LANES // (leaf_count * sub_count)
-        rank = lax.axis_index("leaf") * sub_count + place
+        size = skel * LANES // count
+        rank = lax.axis_index("leaf") * sub_count + lax.axis_index("sub")
         root = lax.dynamic_slice_in_dim(node.reshape(-1), rank * size, size, 0)
-    near = near_call(
-        near_lists, near_counts, rows, acc,
-        [(late_base, single, [late]), (late_beside_base, single, [late_beside])],
-        dim, True, "near_last",
-    )
     return near.reshape(npts, LANES), root
 
 

time: 127 us -> 93.5 us (0.74)
  the two profiles are of different devices: /device:TPU:4 before, /device:TPU:8 now
where the time goes in v1:
time: 93.5 us; the launch traced here: 93.4 us
  Pallas kernels  43.2 us (46%)
  starting transfers between devices  25.4 us (27%)
  waiting for transfers between devices  19.2 us (21%)
  local copies, waits for them, and re-layouts  4.58 us (5%)
  between operations  1.05 us (1%)
    pallas_call x3, Pallas kernels, near_call(): pl.pallas_call(functools.partial(near_kernel, slots=slots, dim=dim, has_a...  24 us
    ppermute x9, starting transfers between devices, send(): return lax.ppermute(x, axes, pairs)  17.3 us
    ppermute x9, waiting for transfers between devices, send(): return lax.ppermute(x, axes, pairs)  16.6 us
    ppermute x7, starting transfers between devices, exchange(): lax.ppermute(x, axes, [(i, i ^ d << shift) for i in range(count)])  8.08 us
    pallas_call x1, Pallas kernels, local_tree_call(): pl.pallas_call(functools.partial(local_tree_kernel, dim=dim), in_specs=[p...  6.86 us
    pallas_call x1, Pallas kernels, order_call(): pl.pallas_call(order_kernel, in_specs=[pl.BlockSpec(memory_space=pltpu.HB...  6.19 us
    pallas_call x3, Pallas kernels, merge_call(): pl.pallas_call(functools.partial(merge_kernel, dim=dim, blocks=blocks, sh...  6.16 us
    unnamed x16, local copies, waits for them, and re-layouts  4.58 us
  transfers between devices with their start and end apart: 16, of which 4 were waited for; matrix products, arithmetic and copies ran while one was open for 0% of the time, Pallas kernels for 38%

profile of v1, /device:TPU:8, one launch (start us, length us, event | category | flops | bytes accessed | tf_op | source)
XLA Modules:
  0.0 93.4 jit_solution(14053503506460109621)
XLA Ops:
  0.6 1.2 %copy-done.2 = bf16[4096,128]{1,0:T(8,128)(2,1)S(1)} copy-done((bf16[4096,128]{1,0:T(8,128)(2,1)S(1)}, bf16[4096,128]{1,0:T(8,128)(2,1)}, u32[]{:S(2)}) %copy-start.2) | copy-done | bytes 1048600
  1.9 1.0 %copy-done.3 = bf16[4096,64]{0,1:T(8,128)(2,1)S(1)} copy-done((bf16[4096,64]{0,1:T(8,128)(2,1)S(1)}, bf16[4096,64]{0,1:T(8,128)(2,1)}, u32[]{:S(2)}) %copy-start.3) | copy-done | bytes 524312
  3.6 6.2 %tree_order.1 = (bf16[8,832,128]{2,1,0:T(8,128)(2,1)S(1)}, bf16[8,512,128]{2,1,0:T(8,128)(2,1)S(1)}) custom-call(bf16[64,4096]{1,0:T(8,128)(2,1)S(1)} %bitcast.4, s32[8,1,512]{2,1,0:T(1,128)S(1)} %bitcast.5, bf16[4096,128]{1,0:T(8,128)(2,1)S(1)} %copy-done.2), custom_call_target="tpu_custom_call" | custom-call | flops 268435456 | bytes 5242880 | tf_op jit(solution)/shard_map/tree_order/pallas_call | solution.py:110
  9.9 3.5 %collective-permute-start = (bf16[8,832,128]{2,1,0:T(8,128)(2,1)S(1)}, bf16[8,832,128]{2,1,0:T(8,128)(2,1)S(1)}, u32[]{:S(2)}, u32[]{:S(2)}) collective-permute-start(bf16[8,832,128]{2,1,0:T(8,128)(2,1)S(1)} %get-tuple-element.37.pack.refs_3_), channel_id=1, source_target_pairs={{3,1},{0,2},{7,5},{4,6},{11,9},{8,10},{15,13},{12,14},{19,17},{16,... | collective-permute-start | bytes 5111816 | tf_op jit(solution)/shard_map/ppermute | solution.py:427
  13.4 3.3 %collective-permute-start.1 = (bf16[8,832,128]{2,1,0:T(8,128)(2,1)S(1)}, bf16[8,832,128]{2,1,0:T(8,128)(2,1)S(1)}, u32[]{:S(2)}, u32[]{:S(2)}) collective-permute-start(bf16[8,832,128]{2,1,0:T(8,128)(2,1)S(1)} %get-tuple-element.37.pack.refs_3_), channel_id=1, source_target_pairs={{3,7},{7,11},{4,0},{11,15},{8,4},{15,19},{12,8},{19,23},{16,12},{2... | collective-permute-start | bytes 5111816 | tf_op jit(solution)/shard_map/ppermute | solution.py:427
  18.3 6.9 %local_tree.1.refs_0_ = f32[208,128]{1,0:T(8,128)S(1)} custom-call(bf16[8,832,128]{2,1,0:T(8,128)(2,1)S(1)} %get-tuple-element.37.pack.refs_3_, bf16[8,512,128]{2,1,0:T(8,128)(2,1)S(1)} %get-tuple-element.29.rows.refs_2_, s32[8,128]{1,0:T(8,128)S(1)} %copy-done.6, s32[255,128]{1,0:T(8,128)S(1)} %copy-done), custom_call_target="tpu_custom_call" | custom-call | flops 536870912 | bytes 3145728 | tf_op jit(solution)/shard_map/local_tree/pallas_call | solution.py:189
  25.8 1.3 %collective-permute-start.5 = (f32[208,128]{1,0:T(8,128)S(1)}, f32[208,128]{1,0:T(8,128)S(1)}, u32[]{:S(2)}, u32[]{:S(2)}) collective-permute-start(f32[208,128]{1,0:T(8,128)S(1)} %local_tree.1.refs_0_), channel_id=1, source_target_pairs={{0,3},{1,2},{2,1},{3,0},{4,7},{5,6},{6,5},{7,4},{8,11},{9,10},{10,... | collective-permute-start | bytes 319496 | tf_op jit(solution)/shard_map/ppermute | solution.py:444
  27.2 8.0 %near_first.1.refs_3_ = f32[8,512,128]{2,1,0:T(8,128)S(1)} custom-call(s32[8,12]{1,0:T(8,128)S(1)} %copy-done.5, s32[8]{0:T(128)S(1)} %copy-done.7, bf16[8,512,128]{2,1,0:T(8,128)(2,1)S(1)} %get-tuple-element.29.rows.refs_2_, bf16[8,832,128]{2,1,0:T(8,128)(2,1)S(1)} %get-tuple-element.37.pack.refs_3_, bf16[8,832,128]{2,1,0:T(8,128)(2,1)S(1)} %collective-permute-done.2.refs_4_), custom_call_target="tpu_custom_call" | custom-call | flops 2147483648 | bytes 7602176 | tf_op jit(solution)/shard_map/near_first/pallas_call | solution.py:391
  36.1 1.6 %collective-permute-done.5.refs_3_ = f32[208,128]{1,0:T(8,128)S(1)} collective-permute-done((f32[208,128]{1,0:T(8,128)S(1)}, f32[208,128]{1,0:T(8,128)S(1)}, u32[]{:S(2)}, u32[]{:S(2)}) %collective-permute-start.5) | collective-permute-done | bytes 106528 | tf_op jit(solution)/shard_map/ppermute | solution.py:444
  37.7 2.2 %tree_merge.3.refs_0_ = f32[208,128]{1,0:T(8,128)S(1)} custom-call(f32[208,128]{1,0:T(8,128)S(1)} %local_tree.1.refs_0_, f32[208,128]{1,0:T(8,128)S(1)} %collective-permute-done.3.refs_1_, f32[208,128]{1,0:T(8,128)S(1)} %collective-permute-done.4.refs_2_, f32[208,128]{1,0:T(8,128)S(1)} %collective-permute-done.5.refs_3_, s32[255,128]{1,0:T(8,128)S(1)} %copy-done.1), custom_call_target="tpu_custom_call" | custom-call | flops 134217728 | bytes 425984 | tf_op jit(solution)/shard_map/tree_merge/pallas_call | solution.py:263
  39.9 1.4 %collective-permute-start.11 = (bf16[8,832,128]{2,1,0:T(8,128)(2,1)S(1)}, bf16[8,832,128]{2,1,0:T(8,128)(2,1)S(1)}, u32[]{:S(2)}, u32[]{:S(2)}) collective-permute-start(bf16[8,832,128]{2,1,0:T(8,128)(2,1)S(1)} %collective-permute-done.1.refs_4_), channel_id=1, source_target_pairs={{0,1},{3,2},{4,5},{7,6},{8,9},{11,10},{12,13},{15,14},{16,17},{19,... | collective-permute-start | bytes 5111816 | tf_op jit(solution)/shard_map/ppermute | solution.py:427
  41.4 1.3 %collective-permute-start.12 = (bf16[8,832,128]{2,1,0:T(8,128)(2,1)S(1)}, bf16[8,832,128]{2,1,0:T(8,128)(2,1)S(1)}, u32[]{:S(2)}, u32[]{:S(2)}) collective-permute-start(bf16[8,832,128]{2,1,0:T(8,128)(2,1)S(1)} %collective-permute-done.refs_5_), channel_id=1, source_target_pairs={{1,0},{2,3},{5,4},{6,7},{9,8},{10,11},{13,12},{14,15},{17,16},{18,... | collective-permute-start | bytes 5111816 | tf_op jit(solution)/shard_map/ppermute | solution.py:427
  43.4 1.5 %collective-permute-start.9 = (bf16[8,832,128]{2,1,0:T(8,128)(2,1)S(1)}, bf16[8,832,128]{2,1,0:T(8,128)(2,1)S(1)}, u32[]{:S(2)}, u32[]{:S(2)}) collective-permute-start(bf16[8,832,128]{2,1,0:T(8,128)(2,1)S(1)} %get-tuple-element.37.pack.refs_3_), channel_id=1, source_target_pairs={{2,0},{1,3},{6,4},{5,7},{10,8},{9,11},{14,12},{13,15},{18,16},{17,... | collective-permute-start | bytes 5111816 | tf_op jit(solution)/shard_map/ppermute | solution.py:427
  44.9 1.6 %collective-permute-start.6 = (f32[208,128]{1,0:T(8,128)S(1)}, f32[208,128]{1,0:T(8,128)S(1)}, u32[]{:S(2)}, u32[]{:S(2)}) collective-permute-start(f32[208,128]{1,0:T(8,128)S(1)} %tree_merge.3.refs_0_), channel_id=1, source_target_pairs={{0,4},{1,5},{2,6},{3,7},{4,0},{5,1},{6,2},{7,3},{8,12},{9,13},{10,... | collective-permute-start | bytes 319496 | tf_op jit(solution)/shard_map/ppermute | solution.py:444
  46.9 1.5 %collective-permute-start.8 = (f32[208,128]{1,0:T(8,128)S(1)}, f32[208,128]{1,0:T(8,128)S(1)}, u32[]{:S(2)}, u32[]{:S(2)}) collective-permute-start(f32[208,128]{1,0:T(8,128)S(1)} %tree_merge.3.refs_0_), channel_id=1, source_target_pairs={{0,12},{1,13},{2,14},{3,15},{4,8},{5,9},{6,10},{7,11},{8,4},{9,5},... | collective-permute-start | bytes 319496 | tf_op jit(solution)/shard_map/ppermute | solution.py:444
  48.5 6.6 %near_second.1.refs_3_ = f32[8,512,128]{2,1,0:T(8,128)S(1)} custom-call(s32[8,12]{1,0:T(8,128)S(1)} %copy-done.5, s32[8]{0:T(128)S(1)} %copy-done.7, bf16[8,512,128]{2,1,0:T(8,128)(2,1)S(1)} %get-tuple-element.29.rows.refs_2_, f32[8,512,128]{2,1,0:T(8,128)S(1)} %near_first.1.refs_3_, bf16[8,832,128]{2,1,0:T(8,128)(2,1)S(1)} %collective-permute-done.1.refs_4_, ...), custom_call_target="tpu_custom_call" | custom-call | flops 2147483648 | bytes 7602176 | tf_op jit(solution)/shard_map/near_second/pallas_call | solution.py:391
  55.1 14.6 %collective-permute-done.9.refs_4_ = bf16[8,832,128]{2,1,0:T(8,128)(2,1)S(1)} collective-permute-done((bf16[8,832,128]{2,1,0:T(8,128)(2,1)S(1)}, bf16[8,832,128]{2,1,0:T(8,128)(2,1)S(1)}, u32[]{:S(2)}, u32[]{:S(2)}) %collective-permute-start.9) | collective-permute-done | bytes 1703968 | tf_op jit(solution)/shard_map/ppermute | solution.py:427
  69.8 4.2 %collective-permute-start.13 = (bf16[8,832,128]{2,1,0:T(8,128)(2,1)S(1)}, bf16[8,832,128]{2,1,0:T(8,128)(2,1)S(1)}, u32[]{:S(2)}, u32[]{:S(2)}) collective-permute-start(bf16[8,832,128]{2,1,0:T(8,128)(2,1)S(1)} %collective-permute-done.9.refs_4_), channel_id=1, source_target_pairs={{0,1},{3,2},{4,5},{7,6},{8,9},{11,10},{12,13},{15,14},{16,17},{19,... | collective-permute-start | bytes 5111816 | tf_op jit(solution)/shard_map/ppermute | solution.py:427
  73.9 1.3 %collective-permute-start.14 = (bf16[8,832,128]{2,1,0:T(8,128)(2,1)S(1)}, bf16[8,832,128]{2,1,0:T(8,128)(2,1)S(1)}, u32[]{:S(2)}, u32[]{:S(2)}) collective-permute-start(bf16[8,832,128]{2,1,0:T(8,128)(2,1)S(1)} %collective-permute-done.10.refs_5_), channel_id=1, source_target_pairs={{1,0},{2,3},{5,4},{6,7},{9,8},{10,11},{13,12},{14,15},{17,16},{18,... | collective-permute-start | bytes 5111816 | tf_op jit(solution)/shard_map/ppermute | solution.py:427
  75.2 2.2 %tree_merge.4.refs_0_ = f32[208,128]{1,0:T(8,128)S(1)} custom-call(f32[208,128]{1,0:T(8,128)S(1)} %tree_merge.3.refs_0_, f32[208,128]{1,0:T(8,128)S(1)} %collective-permute-done.6.refs_1_, f32[208,128]{1,0:T(8,128)S(1)} %collective-permute-done.7.refs_2_, f32[208,128]{1,0:T(8,128)S(1)} %collective-permute-done.8.refs_3_, s32[255,128]{1,0:T(8,128)S(1)} %copy-done.1), custom_call_target="tpu_custom_call" | custom-call | flops 134217728 | bytes 425984 | tf_op jit(solution)/shard_map/tree_merge/pallas_call | solution.py:263
  77.5 1.9 %collective-permute-done.14.refs_7_ = bf16[8,832,128]{2,1,0:T(8,128)(2,1)S(1)} collective-permute-done((bf16[8,832,128]{2,1,0:T(8,128)(2,1)S(1)}, bf16[8,832,128]{2,1,0:T(8,128)(2,1)S(1)}, u32[]{:S(2)}, u32[]{:S(2)}) %collective-permute-start.14) | collective-permute-done | bytes 1703968 | tf_op jit(solution)/shard_map/ppermute | solution.py:427
  79.4 2.6 %collective-permute-start.15 = (f32[208,128]{1,0:T(8,128)S(1)}, f32[208,128]{1,0:T(8,128)S(1)}, u32[]{:S(2)}, u32[]{:S(2)}) collective-permute-start(f32[208,128]{1,0:T(8,128)S(1)} %tree_merge.4.refs_0_), channel_id=1, source_target_pairs={{0,16},{1,17},{2,18},{3,19},{4,20},{5,21},{6,22},{7,23},{8,24},{9,... | collective-permute-start | bytes 319496 | tf_op jit(solution)/shard_map/ppermute | solution.py:444
  82.0 9.5 %near_last.1 = f32[8,512,128]{2,1,0:T(8,128)} custom-call(s32[8,12]{1,0:T(8,128)S(1)} %copy-done.5, s32[8]{0:T(128)S(1)} %copy-done.7, bf16[8,512,128]{2,1,0:T(8,128)(2,1)S(1)} %get-tuple-element.29.rows.refs_2_, f32[8,512,128]{2,1,0:T(8,128)S(1)} %near_second.1.refs_3_, bf16[8,832,128]{2,1,0:T(8,128)(2,1)S(1)} %collective-permute-done.9.refs_4_, ...), custom_call_target="tpu_custom_call" | custom-call | flops 2147483648 | bytes 7602176 | tf_op jit(solution)/shard_map/near_last/pallas_call | solution.py:391
  91.5 1.7 %tree_merge.5 = f32[4,128]{1,0:T(4,128)} custom-call(f32[208,128]{1,0:T(8,128)S(1)} %tree_merge.4.refs_0_, f32[208,128]{1,0:T(8,128)S(1)} %collective-permute-done.15.refs_1_, s32[255,128]{1,0:T(8,128)S(1)} %copy-done.1), custom_call_target="tpu_custom_call" | custom-call | flops 67108864 | bytes 212992 | tf_op jit(solution)/shard_map/tree_merge/pallas_call | solution.py:263
  (32 shorter events, 5.2 us)
Async XLA Ops:
  0.6 1.2 %copy-start.2 = (bf16[4096,128]{1,0:T(8,128)(2,1)S(1)}, bf16[4096,128]{1,0:T(8,128)(2,1)}, u32[]{:S(2)}) copy-start(bf16[4096,128]{1,0:T(8,128)(2,1)} %probes.1) | copy-start | bytes 3145732
  1.9 1.0 %copy-start.3 = (bf16[4096,64]{0,1:T(8,128)(2,1)S(1)}, bf16[4096,64]{0,1:T(8,128)(2,1)}, u32[]{:S(2)}) copy-start(bf16[4096,64]{0,1:T(8,128)(2,1)} %param.7) | copy-start | bytes 1572868
  2.9 0.7 copy-start.4
  3.6 23.6 %copy-start.5 = (s32[8,12]{1,0:T(8,128)S(1)}, s32[8,12]{1,0:T(8,128)}, u32[]{:S(2)}) copy-start(s32[8,12]{1,0:T(8,128)} %refs_0_.5) | copy-start | bytes 1156
  9.8 17.4 %copy-start.7 = (s32[8]{0:T(128)S(1)}, s32[8]{0:T(128)}, u32[]{:S(2)}) copy-start(s32[8]{0:T(128)} %refs_1_.5) | copy-start | bytes 100
  9.8 15.4 %collective-permute-start.2 = (bf16[8,832,128]{2,1,0:T(8,128)(2,1)S(1)}, bf16[8,832,128]{2,1,0:T(8,128)(2,1)S(1)}, u32[]{:S(2)}, u32[]{:S(2)}) collective-permute-start(bf16[8,832,128]{2,1,0:T(8,128)(2,1)S(1)} %get-tuple-element.37.pack.refs_3_), channel_id=1, source_target_pairs={{0,1},{1,0},{2,3},{3,2},{4,5},{5,4},{6,7},{7,6},{8,9},{9,8},{10,11... | collective-permute-start | bytes 5111816 | tf_op jit(solution)/shard_map/ppermute | solution.py:427
  9.9 30.0 %collective-permute-start = (bf16[8,832,128]{2,1,0:T(8,128)(2,1)S(1)}, bf16[8,832,128]{2,1,0:T(8,128)(2,1)S(1)}, u32[]{:S(2)}, u32[]{:S(2)}) collective-permute-start(bf16[8,832,128]{2,1,0:T(8,128)(2,1)S(1)} %get-tuple-element.37.pack.refs_3_), channel_id=1, source_target_pairs={{3,1},{0,2},{7,5},{4,6},{11,9},{8,10},{15,13},{12,14},{19,17},{16,... | collective-permute-start | bytes 5111816 | tf_op jit(solution)/shard_map/ppermute | solution.py:427
  13.4 26.5 %collective-permute-start.1 = (bf16[8,832,128]{2,1,0:T(8,128)(2,1)S(1)}, bf16[8,832,128]{2,1,0:T(8,128)(2,1)S(1)}, u32[]{:S(2)}, u32[]{:S(2)}) collective-permute-start(bf16[8,832,128]{2,1,0:T(8,128)(2,1)S(1)} %get-tuple-element.37.pack.refs_3_), channel_id=1, source_target_pairs={{3,7},{7,11},{4,0},{11,15},{8,4},{15,19},{12,8},{19,23},{16,12},{2... | collective-permute-start | bytes 5111816 | tf_op jit(solution)/shard_map/ppermute | solution.py:427
  16.7 0.9 copy-start
  17.6 0.7 copy-start.6
  25.2 12.5 %copy-start.1 = (s32[255,128]{1,0:T(8,128)S(1)}, s32[255,128]{1,0:T(8,128)}, u32[]{:S(2)}) copy-start(s32[255,128]{1,0:T(8,128)} %refs_2_.1) | copy-start | bytes 391684
  25.2 9.9 %collective-permute-start.3 = (f32[208,128]{1,0:T(8,128)S(1)}, f32[208,128]{1,0:T(8,128)S(1)}, u32[]{:S(2)}, u32[]{:S(2)}) collective-permute-start(f32[208,128]{1,0:T(8,128)S(1)} %local_tree.1.refs_0_), channel_id=1, source_target_pairs={{0,1},{1,0},{2,3},{3,2},{4,5},{5,4},{6,7},{7,6},{8,9},{9,8},{10,11... | collective-permute-start | bytes 319496 | tf_op jit(solution)/shard_map/ppermute | solution.py:444
  25.3 10.8 %collective-permute-start.4 = (f32[208,128]{1,0:T(8,128)S(1)}, f32[208,128]{1,0:T(8,128)S(1)}, u32[]{:S(2)}, u32[]{:S(2)}) collective-permute-start(f32[208,128]{1,0:T(8,128)S(1)} %local_tree.1.refs_0_), channel_id=1, source_target_pairs={{0,2},{1,3},{2,0},{3,1},{4,6},{5,7},{6,4},{7,5},{8,10},{9,11},{10,... | collective-permute-start | bytes 319496 | tf_op jit(solution)/shard_map/ppermute | solution.py:444
  25.8 11.9 %collective-permute-start.5 = (f32[208,128]{1,0:T(8,128)S(1)}, f32[208,128]{1,0:T(8,128)S(1)}, u32[]{:S(2)}, u32[]{:S(2)}) collective-permute-start(f32[208,128]{1,0:T(8,128)S(1)} %local_tree.1.refs_0_), channel_id=1, source_target_pairs={{0,3},{1,2},{2,1},{3,0},{4,7},{5,6},{6,5},{7,4},{8,11},{9,10},{10,... | collective-permute-start | bytes 319496 | tf_op jit(solution)/shard_map/ppermute | solution.py:444
  39.9 6.5 %collective-permute-start.11 = (bf16[8,832,128]{2,1,0:T(8,128)(2,1)S(1)}, bf16[8,832,128]{2,1,0:T(8,128)(2,1)S(1)}, u32[]{:S(2)}, u32[]{:S(2)}) collective-permute-start(bf16[8,832,128]{2,1,0:T(8,128)(2,1)S(1)} %collective-permute-done.1.refs_4_), channel_id=1, source_target_pairs={{0,1},{3,2},{4,5},{7,6},{8,9},{11,10},{12,13},{15,14},{16,17},{19,... | collective-permute-start | bytes 5111816 | tf_op jit(solution)/shard_map/ppermute | solution.py:427
  41.4 5.6 %collective-permute-start.12 = (bf16[8,832,128]{2,1,0:T(8,128)(2,1)S(1)}, bf16[8,832,128]{2,1,0:T(8,128)(2,1)S(1)}, u32[]{:S(2)}, u32[]{:S(2)}) collective-permute-start(bf16[8,832,128]{2,1,0:T(8,128)(2,1)S(1)} %collective-permute-done.refs_5_), channel_id=1, source_target_pairs={{1,0},{2,3},{5,4},{6,7},{9,8},{10,11},{13,12},{14,15},{17,16},{18,... | collective-permute-start | bytes 5111816 | tf_op jit(solution)/shard_map/ppermute | solution.py:427
  42.7 12.5 %collective-permute-start.10 = (bf16[8,832,128]{2,1,0:T(8,128)(2,1)S(1)}, bf16[8,832,128]{2,1,0:T(8,128)(2,1)S(1)}, u32[]{:S(2)}, u32[]{:S(2)}) collective-permute-start(bf16[8,832,128]{2,1,0:T(8,128)(2,1)S(1)} %collective-permute-done.refs_5_), channel_id=1, source_target_pairs={{1,5},{5,9},{6,2},{9,13},{10,6},{13,17},{14,10},{17,21},{18,14},{2... | collective-permute-start | bytes 5111816 | tf_op jit(solution)/shard_map/ppermute | solution.py:427
  43.4 26.3 %collective-permute-start.9 = (bf16[8,832,128]{2,1,0:T(8,128)(2,1)S(1)}, bf16[8,832,128]{2,1,0:T(8,128)(2,1)S(1)}, u32[]{:S(2)}, u32[]{:S(2)}) collective-permute-start(bf16[8,832,128]{2,1,0:T(8,128)(2,1)S(1)} %get-tuple-element.37.pack.refs_3_), channel_id=1, source_target_pairs={{2,0},{1,3},{6,4},{5,7},{10,8},{9,11},{14,12},{13,15},{18,16},{17,... | collective-permute-start | bytes 5111816 | tf_op jit(solution)/shard_map/ppermute | solution.py:427
  44.9 10.2 %collective-permute-start.6 = (f32[208,128]{1,0:T(8,128)S(1)}, f32[208,128]{1,0:T(8,128)S(1)}, u32[]{:S(2)}, u32[]{:S(2)}) collective-permute-start(f32[208,128]{1,0:T(8,128)S(1)} %tree_merge.3.refs_0_), channel_id=1, source_target_pairs={{0,4},{1,5},{2,6},{3,7},{4,0},{5,1},{6,2},{7,3},{8,12},{9,13},{10,... | collective-permute-start | bytes 319496 | tf_op jit(solution)/shard_map/ppermute | solution.py:444
  46.5 8.6 %collective-permute-start.7 = (f32[208,128]{1,0:T(8,128)S(1)}, f32[208,128]{1,0:T(8,128)S(1)}, u32[]{:S(2)}, u32[]{:S(2)}) collective-permute-start(f32[208,128]{1,0:T(8,128)S(1)} %tree_merge.3.refs_0_), channel_id=1, source_target_pairs={{0,8},{1,9},{2,10},{3,11},{4,12},{5,13},{6,14},{7,15},{8,0},{9,1},... | collective-permute-start | bytes 319496 | tf_op jit(solution)/shard_map/ppermute | solution.py:444
  46.9 8.2 %collective-permute-start.8 = (f32[208,128]{1,0:T(8,128)S(1)}, f32[208,128]{1,0:T(8,128)S(1)}, u32[]{:S(2)}, u32[]{:S(2)}) collective-permute-start(f32[208,128]{1,0:T(8,128)S(1)} %tree_merge.3.refs_0_), channel_id=1, source_target_pairs={{0,12},{1,13},{2,14},{3,15},{4,8},{5,9},{6,10},{7,11},{8,4},{9,5},... | collective-permute-start | bytes 319496 | tf_op jit(solution)/shard_map/ppermute | solution.py:444
  69.8 7.7 %collective-permute-start.13 = (bf16[8,832,128]{2,1,0:T(8,128)(2,1)S(1)}, bf16[8,832,128]{2,1,0:T(8,128)(2,1)S(1)}, u32[]{:S(2)}, u32[]{:S(2)}) collective-permute-start(bf16[8,832,128]{2,1,0:T(8,128)(2,1)S(1)} %collective-permute-done.9.refs_4_), channel_id=1, source_target_pairs={{0,1},{3,2},{4,5},{7,6},{8,9},{11,10},{12,13},{15,14},{16,17},{19,... | collective-permute-start | bytes 5111816 | tf_op jit(solution)/shard_map/ppermute | solution.py:427
  73.9 5.5 %collective-permute-start.14 = (bf16[8,832,128]{2,1,0:T(8,128)(2,1)S(1)}, bf16[8,832,128]{2,1,0:T(8,128)(2,1)S(1)}, u32[]{:S(2)}, u32[]{:S(2)}) collective-permute-start(bf16[8,832,128]{2,1,0:T(8,128)(2,1)S(1)} %collective-permute-done.10.refs_5_), channel_id=1, source_target_pairs={{1,0},{2,3},{5,4},{6,7},{9,8},{10,11},{13,12},{14,15},{17,16},{18,... | collective-permute-start | bytes 5111816 | tf_op jit(solution)/shard_map/ppermute | solution.py:427
  79.4 12.1 %collective-permute-start.15 = (f32[208,128]{1,0:T(8,128)S(1)}, f32[208,128]{1,0:T(8,128)S(1)}, u32[]{:S(2)}, u32[]{:S(2)}) collective-permute-start(f32[208,128]{1,0:T(8,128)S(1)} %tree_merge.4.refs_0_), channel_id=1, source_target_pairs={{0,16},{1,17},{2,18},{3,19},{4,20},{5,21},{6,22},{7,23},{8,24},{9,... | collective-permute-start | bytes 319496 | tf_op jit(solution)/shard_map/ppermute | solution.py:444

commit v2 on v1

--- a/solution.py
+++ b/solution.py
@@ -69,57 +69,63 @@
     return dot(m_hi, s_hi) + (dot(m_hi, s_lo) + dot(m_lo, s_hi))
 
 
-def order_kernel(points_t, order, probes, pack, rows, points_in, order_in, sems):
+def order_kernel(points_t, order, probes, pack, rows, points_in, order_in, forms_out, rows_out, sems):
     dim = points_t.shape[0]
     many, leaf = rows.shape[:2]
     held = dim + 16
-    order_copy = pltpu.make_async_copy(order, order_in, sems.at[0])
-    order_copy.start()
-    point_copies, probe_copies = [], []
-    for b in range(many):
-        span = pl.ds(b * leaf, leaf)
-        copy = pltpu.make_async_copy(points_t.at[:, span], points_in.at[b], sems.at[1 + b])
+
+    def begin(source, target, place):
+        copy = pltpu.make_async_copy(source, target, sems.at[place])
         copy.start()
-        point_copies.append(copy)
-    for b in range(many):
-        span = pl.ds(b * leaf, leaf)
-        copy = pltpu.make_async_copy(
-            probes.at[span], pack.at[b, pl.ds(0, leaf)], sems.at[1 + many + b]
-        )
-        copy.start()
-        probe_copies.append(copy)
+        return copy
+
+    order_copy = begin(order, order_in, 0)
+    arrivals = [
+        begin(points_t.at[:, pl.ds(b * leaf, leaf)], points_in.at[b], 1 + b) for b in range(many)
+    ]
+    leaving = [
+        begin(probes.at[pl.ds(b * leaf, leaf)], pack.at[b, pl.ds(0, leaf)], 1 + many + b)
+        for b in range(many)
+    ]
     to_rows = form_map(dim, LANES)
     order_copy.wait()
     for b in range(many):
         picks = onehot_in(order_in[b], leaf)
-        point_copies[b].wait()
+        arrivals[b].wait()
         tree_t = dot(points_in[b], picks).astype(BF16)
         form = jnp.concatenate([tree_t, square_rows(tree_t)], axis=0)
         for i in range(leaf // LANES):
-            pack[b, leaf + i * held : leaf + (i + 1) * held, :] = form[:, i * LANES : (i + 1) * LANES]
+            forms_out[b, i * held : (i + 1) * held, :] = form[:, i * LANES : (i + 1) * LANES]
         form = jnp.concatenate([form, jnp.zeros((LANES - held, leaf), BF16)], axis=0)
-        rows[b] = dot_t(form, to_rows).astype(BF16)
-    for copy in probe_copies:
+        rows_out[b] = dot_t(form, to_rows).astype(BF16)
+        target = pack.at[b, pl.ds(leaf, leaf // LANES * held)]
+        leaving.append(begin(forms_out.at[b], target, 1 + 2 * many + b))
+        leaving.append(begin(rows_out.at[b], rows.at[b], 1 + 3 * many + b))
+    for copy in leaving:
         copy.wait()
 
 
 def order_call(points_t, order, probes, blocks):
     dim, npts = points_t.shape
     leaf = npts // blocks
-    packed = leaf + leaf // LANES * (dim + 16)
+    formed = leaf // LANES * (dim + 16)
+    hbm = pl.BlockSpec(memory_space=pltpu.HBM)
     return pl.pallas_call(
         order_kernel,
-        in_specs=[pl.BlockSpec(memory_space=pltpu.HBM)] * 3,
+        in_specs=[hbm] * 3,
+        out_specs=[hbm] * 2,
         out_shape=[
-            jax.ShapeDtypeStruct((blocks, packed, LANES), BF16),
+            jax.ShapeDtypeStruct((blocks, leaf + formed, LANES), BF16),
             jax.ShapeDtypeStruct((blocks, leaf, LANES), BF16),
         ],
         scratch_shapes=[
             pltpu.VMEM((blocks, dim, leaf), BF16),
             pltpu.VMEM((blocks, 1, leaf), jnp.int32),
-            pltpu.SemaphoreType.DMA((1 + 2 * blocks,)),
-        ],
-        compiler_params=pltpu.CompilerParams(vmem_limit_bytes=VMEM_BYTES),
+            pltpu.VMEM((blocks, formed, LANES), BF16),
+            pltpu.VMEM((blocks, leaf, LANES), BF16),
+            pltpu.SemaphoreType.DMA((1 + 4 * blocks,)),
+        ],
+        compiler_params=pltpu.CompilerParams(vmem_limit_bytes=60 * 1024 * 1024),
         cost_estimate=pl.CostEstimate(
             flops=blocks * 2 * leaf * leaf * dim, bytes_accessed=10 * npts * LANES, transcendentals=0
         ),
@@ -454,26 +460,30 @@
     def tie(*values):
         return lax.optimization_barrier(values)
 
-    beside, node = tie(beside, node)
+    own_pack, node = tie(pack, node)
     parts = exchange(node, 0, sub_bits)
     acc = near_call(
         near_lists, near_counts, rows, None,
-        [(own_base, single, [pack]), (beside_base, single, [beside])],
+        [(own_base, single, [own_pack])],
         dim, False, "near_first",
     )
 
-    *parts, acc = tie(*parts, acc)
+    *parts, inner_pack, outer_across, outer_next, acc = tie(
+        *parts, own_pack, outer_across, outer_next, acc
+    )
+    inner_across = send(inner_pack, [(2, 0, 0), (1, 0, 3)])
+    forwarded = send(outer_across, [(1, 1, 1), (2, -1, 2)])
     node = merge_call(parts, merge_sets, dim, blocks, 0)
-    inner_pack, outer_across, outer_next, node = tie(pack, outer_across, outer_next, node)
     shift, stage_bits = sub_bits, min(2, bits - sub_bits)
     parts = exchange(node, shift, stage_bits)
-    inner_across = send(inner_pack, [(2, 0, 0), (1, 0, 3)])
-    forwarded = send(outer_across, [(1, 1, 1), (2, -1, 2)])
+    outer_next, outer_across, node = tie(outer_next, outer_across, node)
     next_beside = send(outer_next, from_edge)
     across_beside = send(outer_across, from_inner)
+    beside, node = tie(beside, node)
     acc = near_call(
         near_lists, near_counts, rows, acc,
         [
+            (beside_base, single, [beside]),
             (early_base, edge_first, [outer_next, outer_across]),
             (early_beside_base, edge_second, [next_beside, across_beside]),
         ],

time: 93.5 us -> 118 us (1.26)
  the two profiles are of different devices: /device:TPU:8 before, /device:TPU:0 now
where the time goes in v2:
time: 118 us
  Pallas kernels  69.5 us (59%)
  starting transfers between devices  31.1 us (26%)
  waiting for transfers between devices  13.4 us (11%)
  local copies, waits for them, and re-layouts  2.83 us (2%)
    pallas_call x1, Pallas kernels, order_call(): pl.pallas_call(order_kernel, in_specs=[hbm] * 3, out_specs=[hbm] * 2, out...  33.2 us
    pallas_call x3, Pallas kernels, near_call(): pl.pallas_call(functools.partial(near_kernel, slots=slots, dim=dim, has_a...  21.8 us
    ppermute x9, starting transfers between devices, send(): return lax.ppermute(x, axes, pairs)  19.4 us
    ppermute x9, waiting for transfers between devices, send(): return lax.ppermute(x, axes, pairs)  11.7 us
    ppermute x7, starting transfers between devices, exchange(): lax.ppermute(x, axes, [(i, i ^ d << shift) for i in range(count)])  11.6 us
    pallas_call x1, Pallas kernels, local_tree_call(): pl.pallas_call(functools.partial(local_tree_kernel, dim=dim), in_specs=[p...  8.31 us
    pallas_call x3, Pallas kernels, merge_call(): pl.pallas_call(functools.partial(merge_kernel, dim=dim, blocks=blocks, sh...  6.19 us
    unnamed x14, local copies, waits for them, and re-layouts  2.83 us
  transfers between devices with their start and end apart: 16, of which 4 were waited for; matrix products, arithmetic and copies ran while one was open for 0% of the time, Pallas kernels for 29%

profile of v2, /device:TPU:0, one launch (start us, length us, event | category | flops | bytes accessed | tf_op | source)
XLA Modules:
  0.0 117.9 jit_solution(11343844549947817895)
XLA Ops:
  0.6 33.2 %tree_order.1 = (bf16[8,832,128]{2,1,0:T(8,128)(2,1)}, bf16[8,512,128]{2,1,0:T(8,128)(2,1)}) custom-call(bf16[64,4096]{1,0:T(8,128)(2,1)} %bitcast.5, s32[8,1,512]{2,1,0:T(1,128)} %bitcast.6, bf16[4096,128]{1,0:T(8,128)(2,1)} %probes.1), custom_call_target="tpu_custom_call" | custom-call | flops 268435456 | bytes 5242880 | tf_op jit(solution)/shard_map/tree_order/pallas_call | solution.py:113
  33.9 5.0 %collective-permute-start.3 = (bf16[8,832,128]{2,1,0:T(8,128)(2,1)}, bf16[8,832,128]{2,1,0:T(8,128)(2,1)S(1)}, u32[]{:S(2)}, u32[]{:S(2)}) collective-permute-start(bf16[8,832,128]{2,1,0:T(8,128)(2,1)} %get-tuple-element.37.pack.refs_3_), channel_id=1, source_target_pairs={{3,1},{0,2},{7,5},{4,6},{11,9},{8,10},{15,13},{12,14},{19,17},{16,... | collective-permute-start | bytes 5111816 | tf_op jit(solution)/shard_map/ppermute | solution.py:433
  38.8 1.3 %collective-permute-start.4 = (bf16[8,832,128]{2,1,0:T(8,128)(2,1)}, bf16[8,832,128]{2,1,0:T(8,128)(2,1)S(1)}, u32[]{:S(2)}, u32[]{:S(2)}) collective-permute-start(bf16[8,832,128]{2,1,0:T(8,128)(2,1)} %get-tuple-element.37.pack.refs_3_), channel_id=1, source_target_pairs={{3,7},{7,11},{4,0},{11,15},{8,4},{15,19},{12,8},{19,23},{16,12},{2... | collective-permute-start | bytes 5111816 | tf_op jit(solution)/shard_map/ppermute | solution.py:433
  40.2 1.2 %copy-done = bf16[8,512,128]{2,1,0:T(8,128)(2,1)S(1)} copy-done((bf16[8,512,128]{2,1,0:T(8,128)(2,1)S(1)}, bf16[8,512,128]{2,1,0:T(8,128)(2,1)}, u32[]{:S(2)}) %copy-start) | copy-done | bytes 1048600
  43.0 8.3 %local_tree.1.refs_0_ = f32[208,128]{1,0:T(8,128)S(1)} custom-call(bf16[8,832,128]{2,1,0:T(8,128)(2,1)} %get-tuple-element.37.pack.refs_3_, bf16[8,512,128]{2,1,0:T(8,128)(2,1)S(1)} %copy-done, s32[8,128]{1,0:T(8,128)S(1)} %copy-done.6, s32[255,128]{1,0:T(8,128)S(1)} %copy-done.2), custom_call_target="tpu_custom_call" | custom-call | flops 536870912 | bytes 3145728 | tf_op jit(solution)/shard_map/local_tree/pallas_call | solution.py:195
  51.4 2.0 %collective-permute-start.1 = (f32[208,128]{1,0:T(8,128)S(1)}, f32[208,128]{1,0:T(8,128)S(1)}, u32[]{:S(2)}, u32[]{:S(2)}) collective-permute-start(f32[208,128]{1,0:T(8,128)S(1)} %local_tree.1.refs_0_), channel_id=1, source_target_pairs={{0,2},{1,3},{2,0},{3,1},{4,6},{5,7},{6,4},{7,5},{8,10},{9,11},{10,... | collective-permute-start | bytes 319496 | tf_op jit(solution)/shard_map/ppermute | solution.py:450
  53.4 7.6 %near_first.1.refs_3_ = f32[8,512,128]{2,1,0:T(8,128)S(1)} custom-call(s32[8,12]{1,0:T(8,128)S(1)} %copy-done.4, s32[8]{0:T(128)S(1)} %copy-done.5, bf16[8,512,128]{2,1,0:T(8,128)(2,1)S(1)} %copy-done, bf16[8,832,128]{2,1,0:T(8,128)(2,1)} %get-tuple-element.37.pack.refs_3_), custom_call_target="tpu_custom_call" | custom-call | flops 1073741824 | bytes 5898240 | tf_op jit(solution)/shard_map/near_first/pallas_call | solution.py:397
  61.7 1.1 collective-permute-done.2.refs_3_
  62.8 2.2 %tree_merge.3.refs_0_ = f32[208,128]{1,0:T(8,128)S(1)} custom-call(f32[208,128]{1,0:T(8,128)S(1)} %local_tree.1.refs_0_, f32[208,128]{1,0:T(8,128)S(1)} %collective-permute-done.refs_1_, f32[208,128]{1,0:T(8,128)S(1)} %collective-permute-done.1.refs_2_, f32[208,128]{1,0:T(8,128)S(1)} %collective-permute-done.2.refs_3_, s32[255,128]{1,0:T(8,128)S(1)} %copy-done.3), custom_call_target="tpu_custom_call" | custom-call | flops 134217728 | bytes 425984 | tf_op jit(solution)/shard_map/tree_merge/pallas_call | solution.py:269
  65.1 1.4 %collective-permute-start.11 = (bf16[8,832,128]{2,1,0:T(8,128)(2,1)S(1)}, bf16[8,832,128]{2,1,0:T(8,128)(2,1)S(1)}, u32[]{:S(2)}, u32[]{:S(2)}) collective-permute-start(bf16[8,832,128]{2,1,0:T(8,128)(2,1)S(1)} %collective-permute-done.4.refs_5_), channel_id=1, source_target_pairs={{0,1},{3,2},{4,5},{7,6},{8,9},{11,10},{12,13},{15,14},{16,17},{19,... | collective-permute-start | bytes 5111816 | tf_op jit(solution)/shard_map/ppermute | solution.py:433
  66.5 1.3 %collective-permute-start.12 = (bf16[8,832,128]{2,1,0:T(8,128)(2,1)S(1)}, bf16[8,832,128]{2,1,0:T(8,128)(2,1)S(1)}, u32[]{:S(2)}, u32[]{:S(2)}) collective-permute-start(bf16[8,832,128]{2,1,0:T(8,128)(2,1)S(1)} %collective-permute-done.3.refs_6_), channel_id=1, source_target_pairs={{1,0},{2,3},{5,4},{6,7},{9,8},{10,11},{13,12},{14,15},{17,16},{18,... | collective-permute-start | bytes 5111816 | tf_op jit(solution)/shard_map/ppermute | solution.py:433
  67.8 1.3 %collective-permute-start.8 = (bf16[8,832,128]{2,1,0:T(8,128)(2,1)}, bf16[8,832,128]{2,1,0:T(8,128)(2,1)S(1)}, u32[]{:S(2)}, u32[]{:S(2)}) collective-permute-start(bf16[8,832,128]{2,1,0:T(8,128)(2,1)} %get-tuple-element.37.pack.refs_3_), channel_id=1, source_target_pairs={{2,0},{1,3},{6,4},{5,7},{10,8},{9,11},{14,12},{13,15},{18,16},{17,... | collective-permute-start | bytes 5111816 | tf_op jit(solution)/shard_map/ppermute | solution.py:433
  69.9 2.4 %collective-permute-start.5 = (f32[208,128]{1,0:T(8,128)S(1)}, f32[208,128]{1,0:T(8,128)S(1)}, u32[]{:S(2)}, u32[]{:S(2)}) collective-permute-start(f32[208,128]{1,0:T(8,128)S(1)} %tree_merge.3.refs_0_), channel_id=1, source_target_pairs={{0,4},{1,5},{2,6},{3,7},{4,0},{5,1},{6,2},{7,3},{8,12},{9,13},{10,... | collective-permute-start | bytes 319496 | tf_op jit(solution)/shard_map/ppermute | solution.py:450
  72.2 1.6 %collective-permute-start.6 = (f32[208,128]{1,0:T(8,128)S(1)}, f32[208,128]{1,0:T(8,128)S(1)}, u32[]{:S(2)}, u32[]{:S(2)}) collective-permute-start(f32[208,128]{1,0:T(8,128)S(1)} %tree_merge.3.refs_0_), channel_id=1, source_target_pairs={{0,8},{1,9},{2,10},{3,11},{4,12},{5,13},{6,14},{7,15},{8,0},{9,1},... | collective-permute-start | bytes 319496 | tf_op jit(solution)/shard_map/ppermute | solution.py:450
  73.8 1.5 %collective-permute-start.7 = (f32[208,128]{1,0:T(8,128)S(1)}, f32[208,128]{1,0:T(8,128)S(1)}, u32[]{:S(2)}, u32[]{:S(2)}) collective-permute-start(f32[208,128]{1,0:T(8,128)S(1)} %tree_merge.3.refs_0_), channel_id=1, source_target_pairs={{0,12},{1,13},{2,14},{3,15},{4,8},{5,9},{6,10},{7,11},{8,4},{9,5},... | collective-permute-start | bytes 319496 | tf_op jit(solution)/shard_map/ppermute | solution.py:450
  75.3 7.2 %near_second.1.refs_3_ = f32[8,512,128]{2,1,0:T(8,128)S(1)} custom-call(s32[8,12]{1,0:T(8,128)S(1)} %copy-done.4, s32[8]{0:T(128)S(1)} %copy-done.5, bf16[8,512,128]{2,1,0:T(8,128)(2,1)S(1)} %copy-done.1, f32[8,512,128]{2,1,0:T(8,128)S(1)} %near_first.1.refs_3_, bf16[8,832,128]{2,1,0:T(8,128)(2,1)S(1)} %collective-permute-done.10.refs_4_, ...), custom_call_target="tpu_custom_call" | custom-call | flops 3221225472 | bytes 9306112 | tf_op jit(solution)/shard_map/near_second/pallas_call | solution.py:397
  82.6 9.7 %collective-permute-done.8.refs_4_ = bf16[8,832,128]{2,1,0:T(8,128)(2,1)S(1)} collective-permute-done((bf16[8,832,128]{2,1,0:T(8,128)(2,1)}, bf16[8,832,128]{2,1,0:T(8,128)(2,1)S(1)}, u32[]{:S(2)}, u32[]{:S(2)}) %collective-permute-start.8) | collective-permute-done | bytes 1703968 | tf_op jit(solution)/shard_map/ppermute | solution.py:433
  92.3 7.1 %collective-permute-start.13 = (bf16[8,832,128]{2,1,0:T(8,128)(2,1)S(1)}, bf16[8,832,128]{2,1,0:T(8,128)(2,1)S(1)}, u32[]{:S(2)}, u32[]{:S(2)}) collective-permute-start(bf16[8,832,128]{2,1,0:T(8,128)(2,1)S(1)} %collective-permute-done.8.refs_4_), channel_id=1, source_target_pairs={{0,1},{3,2},{4,5},{7,6},{8,9},{11,10},{12,13},{15,14},{16,17},{19,... | collective-permute-start | bytes 5111816 | tf_op jit(solution)/shard_map/ppermute | solution.py:433
  99.4 1.3 %collective-permute-start.14 = (bf16[8,832,128]{2,1,0:T(8,128)(2,1)S(1)}, bf16[8,832,128]{2,1,0:T(8,128)(2,1)S(1)}, u32[]{:S(2)}, u32[]{:S(2)}) collective-permute-start(bf16[8,832,128]{2,1,0:T(8,128)(2,1)S(1)} %collective-permute-done.9.refs_5_), channel_id=1, source_target_pairs={{1,0},{2,3},{5,4},{6,7},{9,8},{10,11},{13,12},{14,15},{17,16},{18,... | collective-permute-start | bytes 5111816 | tf_op jit(solution)/shard_map/ppermute | solution.py:433
  100.7 2.2 %tree_merge.4.refs_0_ = f32[208,128]{1,0:T(8,128)S(1)} custom-call(f32[208,128]{1,0:T(8,128)S(1)} %tree_merge.3.refs_0_, f32[208,128]{1,0:T(8,128)S(1)} %collective-permute-done.5.refs_1_, f32[208,128]{1,0:T(8,128)S(1)} %collective-permute-done.6.refs_2_, f32[208,128]{1,0:T(8,128)S(1)} %collective-permute-done.7.refs_3_, s32[255,128]{1,0:T(8,128)S(1)} %copy-done.3), custom_call_target="tpu_custom_call" | custom-call | flops 134217728 | bytes 425984 | tf_op jit(solution)/shard_map/tree_merge/pallas_call | solution.py:269
  102.9 1.9 %collective-permute-done.14.refs_7_ = bf16[8,832,128]{2,1,0:T(8,128)(2,1)S(1)} collective-permute-done((bf16[8,832,128]{2,1,0:T(8,128)(2,1)S(1)}, bf16[8,832,128]{2,1,0:T(8,128)(2,1)S(1)}, u32[]{:S(2)}, u32[]{:S(2)}) %collective-permute-start.14) | collective-permute-done | bytes 1703968 | tf_op jit(solution)/shard_map/ppermute | solution.py:433
  104.8 4.2 %collective-permute-start.15 = (f32[208,128]{1,0:T(8,128)S(1)}, f32[208,128]{1,0:T(8,128)S(1)}, u32[]{:S(2)}, u32[]{:S(2)}) collective-permute-start(f32[208,128]{1,0:T(8,128)S(1)} %tree_merge.4.refs_0_), channel_id=1, source_target_pairs={{0,16},{1,17},{2,18},{3,19},{4,20},{5,21},{6,22},{7,23},{8,24},{9,... | collective-permute-start | bytes 319496 | tf_op jit(solution)/shard_map/ppermute | solution.py:450
  109.0 7.0 %near_last.1 = f32[8,512,128]{2,1,0:T(8,128)} custom-call(s32[8,12]{1,0:T(8,128)S(1)} %copy-done.4, s32[8]{0:T(128)S(1)} %copy-done.5, bf16[8,512,128]{2,1,0:T(8,128)(2,1)S(1)} %copy-done.1, f32[8,512,128]{2,1,0:T(8,128)S(1)} %near_second.1.refs_3_, bf16[8,832,128]{2,1,0:T(8,128)(2,1)S(1)} %collective-permute-done.8.refs_4_, ...), custom_call_target="tpu_custom_call" | custom-call | flops 2147483648 | bytes 7602176 | tf_op jit(solution)/shard_map/near_last/pallas_call | solution.py:397
  116.0 1.7 %tree_merge.5 = f32[4,128]{1,0:T(4,128)} custom-call(f32[208,128]{1,0:T(8,128)S(1)} %tree_merge.4.refs_0_, f32[208,128]{1,0:T(8,128)S(1)} %collective-permute-done.15.refs_1_, s32[255,128]{1,0:T(8,128)S(1)} %copy-done.3), custom_call_target="tpu_custom_call" | custom-call | flops 67108864 | bytes 212992 | tf_op jit(solution)/shard_map/tree_merge/pallas_call | solution.py:269
  (30 shorter events, 3.2 us)
Async XLA Ops:
  0.6 52.7 %copy-start.4 = (s32[8,12]{1,0:T(8,128)S(1)}, s32[8,12]{1,0:T(8,128)}, u32[]{:S(2)}) copy-start(s32[8,12]{1,0:T(8,128)} %refs_0_.5) | copy-start | bytes 1156
  33.8 19.5 %copy-start.5 = (s32[8]{0:T(128)S(1)}, s32[8]{0:T(128)}, u32[]{:S(2)}) copy-start(s32[8]{0:T(128)} %refs_1_.5) | copy-start | bytes 100
  33.9 29.0 %collective-permute-start.3 = (bf16[8,832,128]{2,1,0:T(8,128)(2,1)}, bf16[8,832,128]{2,1,0:T(8,128)(2,1)S(1)}, u32[]{:S(2)}, u32[]{:S(2)}) collective-permute-start(bf16[8,832,128]{2,1,0:T(8,128)(2,1)} %get-tuple-element.37.pack.refs_3_), channel_id=1, source_target_pairs={{3,1},{0,2},{7,5},{4,6},{11,9},{8,10},{15,13},{12,14},{19,17},{16,... | collective-permute-start | bytes 5111816 | tf_op jit(solution)/shard_map/ppermute | solution.py:433
  38.8 24.0 %collective-permute-start.4 = (bf16[8,832,128]{2,1,0:T(8,128)(2,1)}, bf16[8,832,128]{2,1,0:T(8,128)(2,1)S(1)}, u32[]{:S(2)}, u32[]{:S(2)}) collective-permute-start(bf16[8,832,128]{2,1,0:T(8,128)(2,1)} %get-tuple-element.37.pack.refs_3_), channel_id=1, source_target_pairs={{3,7},{7,11},{4,0},{11,15},{8,4},{15,19},{12,8},{19,23},{16,12},{2... | collective-permute-start | bytes 5111816 | tf_op jit(solution)/shard_map/ppermute | solution.py:433
  40.1 1.2 %copy-start = (bf16[8,512,128]{2,1,0:T(8,128)(2,1)S(1)}, bf16[8,512,128]{2,1,0:T(8,128)(2,1)}, u32[]{:S(2)}) copy-start(bf16[8,512,128]{2,1,0:T(8,128)(2,1)} %get-tuple-element.30.rows.refs_2_) | copy-start | bytes 3145732
  41.4 0.9 copy-start.2
  42.3 0.7 copy-start.6
  51.3 11.6 %copy-start.3 = (s32[255,128]{1,0:T(8,128)S(1)}, s32[255,128]{1,0:T(8,128)}, u32[]{:S(2)}) copy-start(s32[255,128]{1,0:T(8,128)} %refs_2_.1) | copy-start | bytes 391684
  51.3 24.0 %copy-start.1 = (bf16[8,512,128]{2,1,0:T(8,128)(2,1)S(1)}, bf16[8,512,128]{2,1,0:T(8,128)(2,1)}, u32[]{:S(2)}) copy-start(bf16[8,512,128]{2,1,0:T(8,128)(2,1)} %get-tuple-element.30.rows.refs_2_) | copy-start | bytes 3145732
  51.3 9.7 %collective-permute-start = (f32[208,128]{1,0:T(8,128)S(1)}, f32[208,128]{1,0:T(8,128)S(1)}, u32[]{:S(2)}, u32[]{:S(2)}) collective-permute-start(f32[208,128]{1,0:T(8,128)S(1)} %local_tree.1.refs_0_), channel_id=1, source_target_pairs={{0,1},{1,0},{2,3},{3,2},{4,5},{5,4},{6,7},{7,6},{8,9},{9,8},{10,11... | collective-permute-start | bytes 319496 | tf_op jit(solution)/shard_map/ppermute | solution.py:450
  51.4 10.3 %collective-permute-start.1 = (f32[208,128]{1,0:T(8,128)S(1)}, f32[208,128]{1,0:T(8,128)S(1)}, u32[]{:S(2)}, u32[]{:S(2)}) collective-permute-start(f32[208,128]{1,0:T(8,128)S(1)} %local_tree.1.refs_0_), channel_id=1, source_target_pairs={{0,2},{1,3},{2,0},{3,1},{4,6},{5,7},{6,4},{7,5},{8,10},{9,11},{10,... | collective-permute-start | bytes 319496 | tf_op jit(solution)/shard_map/ppermute | solution.py:450
  53.4 9.5 %collective-permute-start.2 = (f32[208,128]{1,0:T(8,128)S(1)}, f32[208,128]{1,0:T(8,128)S(1)}, u32[]{:S(2)}, u32[]{:S(2)}) collective-permute-start(f32[208,128]{1,0:T(8,128)S(1)} %local_tree.1.refs_0_), channel_id=1, source_target_pairs={{0,3},{1,2},{2,1},{3,0},{4,7},{5,6},{6,5},{7,4},{8,11},{9,10},{10,... | collective-permute-start | bytes 319496 | tf_op jit(solution)/shard_map/ppermute | solution.py:450
  61.0 8.9 %collective-permute-start.10 = (bf16[8,832,128]{2,1,0:T(8,128)(2,1)}, bf16[8,832,128]{2,1,0:T(8,128)(2,1)S(1)}, u32[]{:S(2)}, u32[]{:S(2)}) collective-permute-start(bf16[8,832,128]{2,1,0:T(8,128)(2,1)} %get-tuple-element.37.pack.refs_3_), channel_id=1, source_target_pairs={{0,1},{1,0},{2,3},{3,2},{4,5},{5,4},{6,7},{7,6},{8,9},{9,8},{10,11... | collective-permute-start | bytes 5111816 | tf_op jit(solution)/shard_map/ppermute | solution.py:433
  65.1 7.2 %collective-permute-start.11 = (bf16[8,832,128]{2,1,0:T(8,128)(2,1)S(1)}, bf16[8,832,128]{2,1,0:T(8,128)(2,1)S(1)}, u32[]{:S(2)}, u32[]{:S(2)}) collective-permute-start(bf16[8,832,128]{2,1,0:T(8,128)(2,1)S(1)} %collective-permute-done.4.refs_5_), channel_id=1, source_target_pairs={{0,1},{3,2},{4,5},{7,6},{8,9},{11,10},{12,13},{15,14},{16,17},{19,... | collective-permute-start | bytes 5111816 | tf_op jit(solution)/shard_map/ppermute | solution.py:433
  66.5 7.3 %collective-permute-start.12 = (bf16[8,832,128]{2,1,0:T(8,128)(2,1)S(1)}, bf16[8,832,128]{2,1,0:T(8,128)(2,1)S(1)}, u32[]{:S(2)}, u32[]{:S(2)}) collective-permute-start(bf16[8,832,128]{2,1,0:T(8,128)(2,1)S(1)} %collective-permute-done.3.refs_6_), channel_id=1, source_target_pairs={{1,0},{2,3},{5,4},{6,7},{9,8},{10,11},{13,12},{14,15},{17,16},{18,... | collective-permute-start | bytes 5111816 | tf_op jit(solution)/shard_map/ppermute | solution.py:433
  67.8 24.5 %collective-permute-start.8 = (bf16[8,832,128]{2,1,0:T(8,128)(2,1)}, bf16[8,832,128]{2,1,0:T(8,128)(2,1)S(1)}, u32[]{:S(2)}, u32[]{:S(2)}) collective-permute-start(bf16[8,832,128]{2,1,0:T(8,128)(2,1)} %get-tuple-element.37.pack.refs_3_), channel_id=1, source_target_pairs={{2,0},{1,3},{6,4},{5,7},{10,8},{9,11},{14,12},{13,15},{18,16},{17,... | collective-permute-start | bytes 5111816 | tf_op jit(solution)/shard_map/ppermute | solution.py:433
  69.1 23.2 %collective-permute-start.9 = (bf16[8,832,128]{2,1,0:T(8,128)(2,1)S(1)}, bf16[8,832,128]{2,1,0:T(8,128)(2,1)S(1)}, u32[]{:S(2)}, u32[]{:S(2)}) collective-permute-start(bf16[8,832,128]{2,1,0:T(8,128)(2,1)S(1)} %collective-permute-done.3.refs_6_), channel_id=1, source_target_pairs={{1,5},{5,9},{6,2},{9,13},{10,6},{13,17},{14,10},{17,21},{18,14},{2... | collective-permute-start | bytes 5111816 | tf_op jit(solution)/shard_map/ppermute | solution.py:433
  69.9 12.7 %collective-permute-start.5 = (f32[208,128]{1,0:T(8,128)S(1)}, f32[208,128]{1,0:T(8,128)S(1)}, u32[]{:S(2)}, u32[]{:S(2)}) collective-permute-start(f32[208,128]{1,0:T(8,128)S(1)} %tree_merge.3.refs_0_), channel_id=1, source_target_pairs={{0,4},{1,5},{2,6},{3,7},{4,0},{5,1},{6,2},{7,3},{8,12},{9,13},{10,... | collective-permute-start | bytes 319496 | tf_op jit(solution)/shard_map/ppermute | solution.py:450
  72.2 10.3 %collective-permute-start.6 = (f32[208,128]{1,0:T(8,128)S(1)}, f32[208,128]{1,0:T(8,128)S(1)}, u32[]{:S(2)}, u32[]{:S(2)}) collective-permute-start(f32[208,128]{1,0:T(8,128)S(1)} %tree_merge.3.refs_0_), channel_id=1, source_target_pairs={{0,8},{1,9},{2,10},{3,11},{4,12},{5,13},{6,14},{7,15},{8,0},{9,1},... | collective-permute-start | bytes 319496 | tf_op jit(solution)/shard_map/ppermute | solution.py:450
  73.8 8.7 %collective-permute-start.7 = (f32[208,128]{1,0:T(8,128)S(1)}, f32[208,128]{1,0:T(8,128)S(1)}, u32[]{:S(2)}, u32[]{:S(2)}) collective-permute-start(f32[208,128]{1,0:T(8,128)S(1)} %tree_merge.3.refs_0_), channel_id=1, source_target_pairs={{0,12},{1,13},{2,14},{3,15},{4,8},{5,9},{6,10},{7,11},{8,4},{9,5},... | collective-permute-start | bytes 319496 | tf_op jit(solution)/shard_map/ppermute | solution.py:450
  92.3 10.6 %collective-permute-start.13 = (bf16[8,832,128]{2,1,0:T(8,128)(2,1)S(1)}, bf16[8,832,128]{2,1,0:T(8,128)(2,1)S(1)}, u32[]{:S(2)}, u32[]{:S(2)}) collective-permute-start(bf16[8,832,128]{2,1,0:T(8,128)(2,1)S(1)} %collective-permute-done.8.refs_4_), channel_id=1, source_target_pairs={{0,1},{3,2},{4,5},{7,6},{8,9},{11,10},{12,13},{15,14},{16,17},{19,... | collective-permute-start | bytes 5111816 | tf_op jit(solution)/shard_map/ppermute | solution.py:433
  99.4 5.5 %collective-permute-start.14 = (bf16[8,832,128]{2,1,0:T(8,128)(2,1)S(1)}, bf16[8,832,128]{2,1,0:T(8,128)(2,1)S(1)}, u32[]{:S(2)}, u32[]{:S(2)}) collective-permute-start(bf16[8,832,128]{2,1,0:T(8,128)(2,1)S(1)} %collective-permute-done.9.refs_5_), channel_id=1, source_target_pairs={{1,0},{2,3},{5,4},{6,7},{9,8},{10,11},{13,12},{14,15},{17,16},{18,... | collective-permute-start | bytes 5111816 | tf_op jit(solution)/shard_map/ppermute | solution.py:433
  104.8 11.2 %collective-permute-start.15 = (f32[208,128]{1,0:T(8,128)S(1)}, f32[208,128]{1,0:T(8,128)S(1)}, u32[]{:S(2)}, u32[]{:S(2)}) collective-permute-start(f32[208,128]{1,0:T(8,128)S(1)} %tree_merge.4.refs_0_), channel_id=1, source_target_pairs={{0,16},{1,17},{2,18},{3,19},{4,20},{5,21},{6,22},{7,23},{8,24},{9,... | collective-permute-start | bytes 319496 | tf_op jit(solution)/shard_map/ppermute | solution.py:450
